TPU v7x, 32 devices: a whole 2x2x4 slice. The times are simulated.
32 devices in a mesh: dp: 8 (over y, x, core), seq: 4 (over z).
Axes of the slice: x: 2, y: 2, z: 4, core: 2. Of those that a mesh axis runs over, the one named last changes fastest.
Arguments:
- tokens: bfloat16 [8, 1024, 1024], P('dp', 'seq'), may hold values from -6 to 6
- noise_steps: int32 [8], P('dp'), may hold values from 0 to 999
- w_qkv: bfloat16 [1024, 3072], P('dp'), may hold values from -0.1875 to 0.1875
- w_out: bfloat16 [1024, 1024], P('dp'), may hold values from -3.5 to 3.5
- w_up: bfloat16 [1024, 4096], P('dp'), may hold values from -0.1875 to 0.1875
- w_down: bfloat16 [4096, 1024], P('dp'), may hold values from -0.09375 to 0.09375
- w_time: bfloat16 [256, 4096], P(None, 'dp'), may hold values from -0.375 to 0.375
- cotangent: bfloat16 [8, 1024, 1024], P('dp', 'seq'), may hold values from -6 to 6
Outputs:
- result: bfloat16 [8, 1024, 1024], P('dp', 'seq')
- grad_tokens: float32 [8, 1024, 1024], P('dp', 'seq')
- grad_qkv: float32 [1024, 3072], P('dp')
- grad_proj: float32 [1024, 1024], P('dp')
- grad_up: float32 [1024, 4096], P('dp')
- grad_down: float32 [4096, 1024], P('dp')
- grad_time: float32 [256, 4096], P(None, 'dp')
All inputs are finite; a program needn't handle non-finite values.
Results may differ from a plain program's by a relative error of at most 0.015.
Values may be sent and summed in bfloat16 or wider, within the bound.
No kernel may reach another device: no remote copies, remote signals or barrier semaphores. Data moves between devices by JAX's collectives and lax.ppermute only.
A program may use at most 192 MiB of HBM per device.

v0:
```python
from functools import partial
import math

import jax
import jax.numpy as jnp
from jax import lax
from jax.sharding import PartitionSpec as P

HEADS = 16
HEAD_DIM = 64
TE = 256


highest = lax.Precision.HIGHEST


def normalize(values_in):
    centered = values_in - jnp.mean(values_in, axis=-1, keepdims=True)
    inverse = lax.rsqrt(jnp.mean(centered * centered, axis=-1, keepdims=True) + 1e-05)
    return (centered * inverse, inverse)


def norm_back(gradient, normed, inverse):
    return inverse * (
        gradient
        - jnp.mean(gradient, axis=-1, keepdims=True)
        - normed * jnp.mean(gradient * normed, axis=-1, keepdims=True)
    )


def time_embedding(noise_step):
    half_dim = TE // 2
    frequency = jnp.exp(-math.log(10000.0) * jnp.arange(half_dim, dtype=jnp.float32) / half_dim)
    angles = noise_step.astype(jnp.float32)[..., None] * frequency
    return jnp.concatenate([jnp.sin(angles), jnp.cos(angles)], axis=-1)


def rotate(values_in, positions, direction):
    half_dim = values_in.shape[-1] // 2
    frequency = jnp.exp(-math.log(10000.0) * jnp.arange(half_dim, dtype=jnp.float32) / half_dim)
    angles = positions[:, None, None] * frequency
    cosine = jnp.cos(angles)
    sine_wave = direction * jnp.sin(angles)
    first_half = values_in[..., :half_dim]
    second_half = values_in[..., half_dim:]
    return jnp.concatenate(
        [
            first_half * cosine - second_half * sine_wave,
            first_half * sine_wave + second_half * cosine,
        ],
        axis=-1,
    )


def attend_forward(packed):
    seq_count, length = (packed.shape[0], packed.shape[1])
    head_view = packed.reshape(seq_count, length, 3, -1, HEAD_DIM)
    score_scale = 1.0 / math.sqrt(HEAD_DIM)
    scores = (
        jnp.einsum(
            "nqhd,nkhd->nhqk",
            head_view[:, :, 0],
            head_view[:, :, 1],
            preferred_element_type=jnp.float32,
        )
        * score_scale
    )
    row_top = jnp.max(scores, axis=-1, keepdims=True)
    exponent = jnp.exp(scores - row_top)
    row_total = jnp.sum(exponent, axis=-1, keepdims=True)
    attn_probs = (exponent / row_total).astype(jnp.bfloat16)
    attended = jnp.einsum(
        "nhqk,nkhd->nqhd", attn_probs, head_view[:, :, 2], preferred_element_type=jnp.float32
    )
    logsum = (row_top + jnp.log(row_total))[..., 0]
    return (attended.astype(jnp.bfloat16).reshape(seq_count, length, 1, -1), logsum, packed)


def head_back(head_item):
    queries, key_rows, values, grad_attn, log_total = head_item
    score_scale = 1.0 / math.sqrt(HEAD_DIM)
    scores = (
        jnp.einsum("nqd,nkd->nqk", queries, key_rows, preferred_element_type=jnp.float32)
        * score_scale
    )
    attn_probs = jnp.exp(scores - log_total[..., None])
    rounded = attn_probs.astype(jnp.bfloat16)
    grad_probs = jnp.einsum("nqd,nkd->nqk", grad_attn, values, preferred_element_type=jnp.float32)
    grad_scores = (
        attn_probs * (grad_probs - jnp.sum(attn_probs * grad_probs, axis=-1, keepdims=True))
    ).astype(jnp.bfloat16)
    grad_queries = (
        jnp.einsum("nqk,nkd->nqd", grad_scores, key_rows, preferred_element_type=jnp.float32)
        * score_scale
    ).astype(jnp.bfloat16)
    grad_keys = (
        jnp.einsum("nqk,nqd->nkd", grad_scores, queries, preferred_element_type=jnp.float32)
        * score_scale
    ).astype(jnp.bfloat16)
    grad_values = jnp.einsum(
        "nqk,nqd->nkd", rounded, grad_attn, preferred_element_type=jnp.float32
    ).astype(jnp.bfloat16)
    return jnp.stack([grad_queries, grad_keys, grad_values], axis=0)


def attend_backward(packed, grad_heads, logsum):
    seq_count, length = (packed.shape[0], packed.shape[1])
    head_view = packed.reshape(seq_count, length, 3, -1, HEAD_DIM)
    queries = jnp.moveaxis(head_view[:, :, 0], 2, 0)
    key_rows = jnp.moveaxis(head_view[:, :, 1], 2, 0)
    values = jnp.moveaxis(head_view[:, :, 2], 2, 0)
    grad_attn = jnp.moveaxis(grad_heads.reshape(seq_count, length, -1, HEAD_DIM), 2, 0)
    log_total = jnp.moveaxis(logsum, 1, 0)
    head_grads = lax.map(head_back, (queries, key_rows, values, grad_attn, log_total))
    return jnp.transpose(head_grads, (2, 3, 1, 0, 4)).reshape(seq_count, length, 3, 1, -1)


def per_device(tokens, noise_steps, w_qkv, w_out, w_up, w_down, w_time, cotangent):
    qkv_all, out_all, up_all, down_all, time_all = (
        lax.all_gather(w_qkv, "dp", axis=0, tiled=True),
        lax.all_gather(w_out, "dp", axis=0, tiled=True),
        lax.all_gather(w_up, "dp", axis=0, tiled=True),
        lax.all_gather(w_down, "dp", axis=0, tiled=True),
        lax.all_gather(w_time, "dp", axis=1, tiled=True),
    )
    seq_count, tok_rows, model_width = tokens.shape
    seq_parts = lax.axis_size("seq")
    positions = (lax.axis_index("seq") * tok_rows + jnp.arange(tok_rows, dtype=jnp.int32)).astype(
        jnp.float32
    )
    time_embed = time_embedding(noise_steps)
    condition = jnp.dot(time_embed, time_all.astype(jnp.float32), precision=highest)
    scale_a, shift_a, scale_b, shift_b = [
        piece_cond[:, None, :] for piece_cond in jnp.split(condition, 4, axis=-1)
    ]
    source = tokens.astype(jnp.float32)
    normed_a, inverse_a = normalize(source)
    input_a = (normed_a * (1.0 + scale_a) + shift_a).astype(jnp.bfloat16)
    projected = jnp.einsum("std,de->ste", input_a, qkv_all, preferred_element_type=jnp.float32)
    head_view = projected.reshape(seq_count, tok_rows, 3, HEADS, HEAD_DIM)
    queries = rotate(head_view[:, :, 0], positions, 1.0)
    key_rows = rotate(head_view[:, :, 1], positions, 1.0)
    packed = jnp.stack([queries, key_rows, head_view[:, :, 2]], axis=2).astype(jnp.bfloat16)
    packed = packed.reshape(seq_count, tok_rows, 3, seq_parts, -1)
    attended, logsum, heads_in = attend_forward(
        lax.all_to_all(packed, "seq", split_axis=3, concat_axis=1, tiled=True)
    )
    mixed_tok = lax.all_to_all(attended, "seq", split_axis=1, concat_axis=2, tiled=True).reshape(
        seq_count, tok_rows, model_width
    )
    middle = source + jnp.einsum(
        "std,de->ste", mixed_tok, out_all, preferred_element_type=jnp.float32
    )
    normed_b, inverse_b = normalize(middle)
    input_b = (normed_b * (1.0 + scale_b) + shift_b).astype(jnp.bfloat16)
    upper = jnp.einsum("std,df->stf", input_b, up_all, preferred_element_type=jnp.float32)
    hidden = jax.nn.gelu(upper, approximate=False).astype(jnp.bfloat16)
    output = (
        middle + jnp.einsum("stf,fd->std", hidden, down_all, preferred_element_type=jnp.float32)
    ).astype(jnp.bfloat16)
    qkv_all, out_all, up_all, down_all, time_all = (
        lax.all_gather(w_qkv, "dp", axis=0, tiled=True),
        lax.all_gather(w_out, "dp", axis=0, tiled=True),
        lax.all_gather(w_up, "dp", axis=0, tiled=True),
        lax.all_gather(w_down, "dp", axis=0, tiled=True),
        lax.all_gather(w_time, "dp", axis=1, tiled=True),
    )
    grad_result = cotangent.astype(jnp.float32)
    grad_down = jnp.einsum("stf,std->fd", hidden, cotangent, preferred_element_type=jnp.float32)
    grad_hidden = jnp.einsum("std,fd->stf", cotangent, down_all, preferred_element_type=jnp.float32)
    gelu_value, gelu_pull = jax.vjp(partial(jax.nn.gelu, approximate=False), upper)
    grad_upper = gelu_pull(grad_hidden)[0].astype(jnp.bfloat16)
    grad_up = jnp.einsum("std,stf->df", input_b, grad_upper, preferred_element_type=jnp.float32)
    grad_in_b = jnp.einsum("stf,df->std", grad_upper, up_all, preferred_element_type=jnp.float32)
    grad_scale_b = jnp.sum(grad_in_b * normed_b, axis=1)
    grad_shift_b = jnp.sum(grad_in_b, axis=1)
    grad_middle = grad_result + norm_back(grad_in_b * (1.0 + scale_b), normed_b, inverse_b)
    grad_branch = grad_middle.astype(jnp.bfloat16)
    grad_proj = jnp.einsum(
        "std,ste->de", mixed_tok, grad_branch, preferred_element_type=jnp.float32
    )
    grad_mixed = jnp.einsum(
        "ste,de->std", grad_branch, out_all, preferred_element_type=jnp.float32
    ).astype(jnp.bfloat16)
    grad_heads = lax.all_to_all(
        grad_mixed.reshape(seq_count, tok_rows, seq_parts, -1),
        "seq",
        split_axis=2,
        concat_axis=1,
        tiled=True,
    )
    grad_packed = attend_backward(heads_in, grad_heads, logsum)
    grad_local = lax.all_to_all(grad_packed, "seq", split_axis=1, concat_axis=3, tiled=True)
    grad_local = grad_local.reshape(seq_count, tok_rows, 3, HEADS, HEAD_DIM)
    grad_queries = rotate(grad_local[:, :, 0].astype(jnp.float32), positions, -1.0).astype(
        jnp.bfloat16
    )
    grad_keys = rotate(grad_local[:, :, 1].astype(jnp.float32), positions, -1.0).astype(
        jnp.bfloat16
    )
    grad_projected = jnp.stack([grad_queries, grad_keys, grad_local[:, :, 2]], axis=2)
    grad_projected = grad_projected.reshape(seq_count, tok_rows, 3 * model_width)
    grad_qkv = jnp.einsum(
        "std,ste->de", input_a, grad_projected, preferred_element_type=jnp.float32
    )
    grad_in_a = jnp.einsum(
        "ste,de->std", grad_projected, qkv_all, preferred_element_type=jnp.float32
    )
    grad_scale_a = jnp.sum(grad_in_a * normed_a, axis=1)
    grad_shift_a = jnp.sum(grad_in_a, axis=1)
    grad_source = grad_middle + norm_back(grad_in_a * (1.0 + scale_a), normed_a, inverse_a)
    grad_condition = jnp.concatenate(
        [grad_scale_a, grad_shift_a, grad_scale_b, grad_shift_b], axis=-1
    )
    grad_time = jnp.dot(time_embed.T, grad_condition, precision=highest)
    first_sum = (
        lax.psum_scatter(grad_qkv, "dp", scatter_dimension=0, tiled=True),
        lax.psum_scatter(grad_proj, "dp", scatter_dimension=0, tiled=True),
        lax.psum_scatter(grad_up, "dp", scatter_dimension=0, tiled=True),
        lax.psum_scatter(grad_down, "dp", scatter_dimension=0, tiled=True),
        lax.psum_scatter(grad_time, "dp", scatter_dimension=1, tiled=True),
    )
    summed = (
        lax.psum(first_sum[0].astype(jnp.bfloat16), "seq").astype(jnp.float32),
        lax.psum(first_sum[1].astype(jnp.bfloat16), "seq").astype(jnp.float32),
        lax.psum(first_sum[2].astype(jnp.bfloat16), "seq").astype(jnp.float32),
        lax.psum(first_sum[3].astype(jnp.bfloat16), "seq").astype(jnp.float32),
        lax.psum(first_sum[4].astype(jnp.bfloat16), "seq").astype(jnp.float32),
    )
    return (output, grad_source, summed[0], summed[1], summed[2], summed[3], summed[4])


def solution(mesh):
    in_specs = (
        P("dp", "seq", None),
        P("dp"),
        P("dp", None),
        P("dp", None),
        P("dp", None),
        P("dp", None),
        P(None, "dp"),
        P("dp", "seq", None),
    )
    out_specs = (
        P("dp", "seq", None),
        P("dp", "seq", None),
        P("dp", None),
        P("dp", None),
        P("dp", None),
        P("dp", None),
        P(None, "dp"),
    )
    return jax.shard_map(
        per_device, mesh=mesh, in_specs=in_specs, out_specs=out_specs, check_vma=False
    )
```

profile of v0, /device:TPU:0, one launch (start us, length us, event | category | flops | bytes accessed | tf_op | source)
XLA Modules:
  0.0 919.5 jit_solution(2636810834563269881)
XLA Ops:
  13.6 27.2 %all-gather.6.cloned.1.call-done = bf16[256,4096]{1,0:T(8,128)(2,1)} async-done(((bf16[256,512]{1,0:T(8,128)(2,1)}), bf16[256,4096]{1,0:T(8,128)(2,1)}) %all-gather.6.cloned.1.call-update) | async-done | bytes 2097168 | tf_op jit(solution)/shard_map/all_gather | solution.py:124
  43.4 44.9 %all-gather.8.cloned.1.call-done = bf16[1024,3072]{1,0:T(8,128)(2,1)} async-done(((bf16[128,3072]{1,0:T(8,128)(2,1)}), bf16[1024,3072]{1,0:T(8,128)(2,1)}) %all-gather.8.cloned.1.call-update) | async-done | bytes 6291472 | tf_op jit(solution)/shard_map/all_gather | solution.py:120
  88.3 8.7 copy.45
  97.0 5.0 convolution_bitcast_fusion
  102.8 42.3 %all_to_all.60 = bf16[1,256,3,4,256]{1,4,2,0,3:T(8,128)(2,1)S(1)} all-to-all(bf16[1,256,3,4,256]{1,4,2,0,3:T(8,128)(2,1)S(1)} %pad_maximum_fusion), channel_id=1, replica_groups=mesh['dp'=8,'seq'=4] {'seq'}, dimensions={3} | all-to-all | bytes 3145728 | tf_op jit(solution)/shard_map/all_to_all | solution.py:146
  147.5 3.0 reshape.715
  150.5 8.1 multiply_reduce_fusion.1
  158.6 8.7 fusion.36
  167.3 7.8 fusion.46
  176.7 3.8 reduce.22
  181.4 3.5 all-to-all-start.1
  184.9 14.1 %all-to-all-done.1 = bf16[4,2,32768]{2,1,0:T(2,128)(2,1)S(1)} async-done(((bf16[4,2,32768]{2,1,0:T(2,128)(2,1)}), bf16[4,2,32768]{2,1,0:T(2,128)(2,1)S(1)}, u32[]{:S(2)}, u32[]{:S(2)}) %all-to-all-start.1) | async-done | bytes 524320 | tf_op jit(solution)/shard_map/all_to_all | solution.py:148
  202.6 16.7 %multiply_convert_fusion.1 = (bf16[256,4096]{1,0:T(8,128)(2,1)}, f32[256,4096]{1,0:T(8,128)}, f32[256,4096]{1,0:T(8,128)}) fusion(bf16[1024,4096]{1,0:T(8,128)(2,1)} %all-gather.12.cloned.1.call-done, f32[1,256,1024]{2,1,0:T(8,128)S(1)} %get-tuple-element.134, f32[1024]{0:T(1024)S(1)} %bitcast.283, f32[1024]{0:T(1024)S(1)} %bitcast.273, ...), kind=kOutput, calls=%fused_computation.46 | convolution fusion | flops 2216951808 | bytes 19933184 | tf_op jit(solution)/shard_map/std,df->stf/dot_general | solution.py:156
  219.3 11.1 %all-gather.14.cloned.1.call-done = bf16[4096,1024]{1,0:T(8,128)(2,1)} async-done(((bf16[512,1024]{1,0:T(8,128)(2,1)}), bf16[4096,1024]{1,0:T(8,128)(2,1)}) %all-gather.14.cloned.1.call-update) | async-done | bytes 8388624 | tf_op jit(solution)/shard_map/all_gather | solution.py:123
  230.4 11.6 %add_convert_fusion = bf16[256,4096]{1,0:T(8,128)(2,1)S(1)} fusion(f32[256,4096]{1,0:T(8,128)} %get-tuple-element.101, f32[256,4096]{1,0:T(8,128)} %get-tuple-element.135, bf16[4096,1024]{1,0:T(8,128)(2,1)} %all-gather.14.cloned.1.call-done, bf16[1,256,1024]{2,1,0:T(8,128)(2,1)S(1)} %copy-done.6), kind=kOutput, calls=%fused_computation.45 | convolution fusion | flops 2162163712 | bytes 19398656 | tf_op jit(solution)/shard_map/std,fd->stf/dot_general | solution.py:170
  249.9 4.6 all-to-all-start.2
  259.7 9.7 %all-to-all-done.2 = bf16[1,256,4,256]{1,3,0,2:T(8,128)(2,1)} async-done(((bf16[1,256,4,256]{1,3,0,2:T(8,128)(2,1)}), bf16[1,256,4,256]{1,3,0,2:T(8,128)(2,1)}, u32[]{:S(2)}, u32[]{:S(2)}) %all-to-all-start.2) | async-done | bytes 524320 | tf_op jit(solution)/shard_map/all_to_all | solution.py:185
  273.2 38.3 %while.10 = (s32[]{:T(128)}, bf16[4,3,1,1024,64]{3,4,0,1,2:T(8,128)(2,1)}, bf16[4,1,1024,64]{2,3,0,1:T(8,128)(2,1)}, bf16[4,1,1024,64]{2,3,0,1:T(8,128)(2,1)}, f...) while((s32[]{:T(128)}, ...), condition=%wide.region_10.11_spmd, body=%wide.region_8.10_spmd.sunk | while | flops 685177856 | bytes 33586780 | solution.py:114
  311.5 4.1 copy.60
  315.7 4.5 all-to-all-start.3
  320.2 47.8 %all-to-all-done.3 = bf16[1,1024,3,1,256]{4,2,3,0,1:T(4,128)(2,1)} async-done(((bf16[1,1024,3,1,256]{4,2,3,0,1:T(4,128)(2,1)}), bf16[1,1024,3,1,256]{4,2,3,0,1:T(4,128)(2,1)}, u32[]{:S(2)}, u32[]{:S(2)}) %all-to-all-start.3) | async-done | bytes 1572896 | tf_op jit(solution)/shard_map/all_to_all | solution.py:193
  370.9 3.0 copy.62
  376.0 5.5 fusion.59
  385.3 8.8 fusion.82
  394.1 10.1 %fusion.100 = f32[1024,4096]{1,0:T(8,128)} fusion(bf16[256,4096]{1,0:T(8,128)(2,1)} %copy-done.9, f32[1,256,1024]{2,1,0:T(8,128)S(1)} %get-tuple-element.134, f32[1024]{0:T(1024)S(1)} %bitcast.284, f32[1024]{0:T(1024)S(1)} %bitcast.277, f32[256]{0:T(256)S(1)} %add_rsqrt_fusion, f32[256]{0:T(256)S(1)} %broadcast_multiply_fusion.6), kind=kOutput, calls=%fused_computation.167 | convolution fusion | flops 2148794368 | bytes 19933184 | tf_op jit(solution)/shard_map/std,stf->df/dot_general | solution.py:173
  405.3 10.2 %fusion.72 = f32[4096,1024]{1,0:T(8,128)} fusion(bf16[256,4096]{1,0:T(8,128)(2,1)} %get-tuple-element.100, bf16[1,256,1024]{2,1,0:T(8,128)(2,1)S(1)} %copy-done.8), kind=kOutput, calls=%fused_computation.113 | convolution fusion | flops 2147483648 | bytes 19398656 | tf_op jit(solution)/shard_map/stf,std->fd/dot_general | solution.py:169
  417.5 17.4 %reduce-scatter.14.cloned.1.call-done = f32[256,512]{1,0:T(8,128)} async-done(((f32[256,4096]{1,0:T(8,128)}), f32[256,512]{1,0:T(8,128)}) %reduce-scatter.14.cloned.1.call-update) | async-done | bytes 524304 | tf_op jit(solution)/shard_map/reduce_scatter | solution.py:221
  436.6 94.2 %reduce-scatter.6.cloned.1.call-done = f32[128,3072]{1,0:T(8,128)} async-done(((f32[1024,3072]{1,0:T(8,128)}), f32[128,3072]{1,0:T(8,128)}) %reduce-scatter.6.cloned.1.call-update) | async-done | bytes 1572880 | tf_op jit(solution)/shard_map/reduce_scatter | solution.py:217
  533.2 117.2 %reduce-scatter.10.cloned.1.call-done = f32[128,4096]{1,0:T(8,128)} async-done(((f32[1024,4096]{1,0:T(8,128)}), f32[128,4096]{1,0:T(8,128)}) %reduce-scatter.10.cloned.1.call-update) | async-done | bytes 2097168 | tf_op jit(solution)/shard_map/reduce_scatter | solution.py:219
  653.1 116.7 %reduce-scatter.12.cloned.1.call-done = f32[512,1024]{1,0:T(8,128)} async-done(((f32[4096,1024]{1,0:T(8,128)}), f32[512,1024]{1,0:T(8,128)}) %reduce-scatter.12.cloned.1.call-update) | async-done | bytes 2097168 | tf_op jit(solution)/shard_map/reduce_scatter | solution.py:220
  772.5 7.2 fusion.45
  781.1 123.0 %all-reduce.3.cloned.1.call-done = (bf16[128,3072]{1,0:T(8,128)(2,1)}, bf16[128,1024]{1,0:T(8,128)(2,1)}, bf16[128,4096]{1,0:T(8,128)(2,1)}, bf16[512,1024]{1,0:T(8,128)(2,1)}, bf16[256,512]{1,0:T(8,128)(2,1)}) async-done(((bf16[128,3072]{1,0:T(8,128)(2,1)}, bf16[128,1024]{1,0:T(8,128)(2,1)}, bf16[128,4096]{1,0:T(8,128)(2,1)}, bf16[512,1024]{1,0:T(8,128)(2,1)}, bf16[256,512]{1,0:T(8,128)(2,1)}), ...) | async-done | bytes 3407888 | tf_op jit(solution)/shard_map/psum | solution.py:224
  (161 shorter events, 103.8 us)
Async XLA Ops:
  7.2 5.3 copy-start.1
  7.2 33.7 %all-gather.6.cloned.1.call-start = ((), (), s32[]{:S(2)}) async-start(), calls=%async_computation.9 | async-start | bytes 2359296 | tf_op jit(solution)/shard_map/all_gather | solution.py:124
  7.9 80.4 %all-gather.8.cloned.1.call-start = ((), (), s32[]{:S(2)}) async-start(), calls=%async_computation.10 | async-start | bytes 7077888 | tf_op jit(solution)/shard_map/all_gather | solution.py:120
  8.7 191.2 %all-gather.10.cloned.1.call-start = ((), (), s32[]{:S(2)}) async-start(), calls=%async_computation.11 | async-start | bytes 2359296 | tf_op jit(solution)/shard_map/all_gather | solution.py:121
  9.4 193.2 %all-gather.12.cloned.1.call-start = ((), (), s32[]{:S(2)}) async-start(), calls=%async_computation.12 | async-start | bytes 9437184 | tf_op jit(solution)/shard_map/all_gather | solution.py:122
  10.0 220.4 %all-gather.14.cloned.1.call-start = ((), (), s32[]{:S(2)}) async-start(), calls=%async_computation.13 | async-start | bytes 9437184 | tf_op jit(solution)/shard_map/all_gather | solution.py:123
  11.3 29.6 %copy-start.16 = (f32[1,128]{1,0:T(1,128)}, f32[1,128]{1,0:T(1,128)S(1)}, u32[]{:S(2)}) copy-start(f32[1,128]{1,0:T(1,128)S(1)} %get-tuple-element.138) | copy-start | bytes 1540
  11.3 29.5 %copy-start.18 = (f32[1,128]{1,0:T(1,128)}, f32[1,128]{1,0:T(1,128)S(1)}, u32[]{:S(2)}) copy-start(f32[1,128]{1,0:T(1,128)S(1)} %get-tuple-element.139) | copy-start | bytes 1540
  43.4 53.6 %copy-start.14 = (f32[1,1024]{1,0:T(1,128)}, f32[1,1024]{1,0:T(1,128)S(1)}, u32[]{:S(2)}) copy-start(f32[1,1024]{1,0:T(1,128)S(1)} %get-tuple-element.125) | copy-start | bytes 12292
  150.5 16.8 %copy-start = (bf16[1,1024,3,4,64]{1,4,3,2,0:T(8,128)(2,1)}, bf16[1,1024,3,4,64]{1,4,3,2,0:T(8,128)(2,1)S(1)}, u32[]{:S(2)}) copy-start(bf16[1,1024,3,4,64]{1,4,3,2,0:T(8,128)(2,1)S(1)} %reshape.715) | copy-start | bytes 4718596
  181.4 17.6 %all-to-all-start.1 = ((bf16[4,2,32768]{2,1,0:T(2,128)(2,1)}), bf16[4,2,32768]{2,1,0:T(2,128)(2,1)S(1)}, u32[]{:S(2)}, u32[]{:S(2)}) async-start(bf16[4,2,32768]{2,1,0:T(2,128)(2,1)} %reshape.735), calls=%async_computation.1 | async-start | bytes 1048576 | tf_op jit(solution)/shard_map/all_to_all | solution.py:148
  202.6 27.8 %copy-start.6 = (bf16[1,256,1024]{2,1,0:T(8,128)(2,1)S(1)}, bf16[1,256,1024]{2,1,0:T(8,128)(2,1)}, u32[]{:S(2)}) copy-start(bf16[1,256,1024]{2,1,0:T(8,128)(2,1)} %param.17) | copy-start | bytes 1572868
  230.4 11.6 %copy-start.20 = (bf16[1024,4096]{1,0:T(8,128)(2,1)S(1)}, bf16[1024,4096]{1,0:T(8,128)(2,1)}, u32[]{:S(2)}) copy-start(bf16[1024,4096]{1,0:T(8,128)(2,1)} %all-gather.12.cloned.1.call-done) | copy-start | bytes 25165828
  242.0 2.6 copy-start.9
  242.1 2.8 copy-start.7
  249.9 19.6 %all-to-all-start.2 = ((bf16[1,256,4,256]{1,3,0,2:T(8,128)(2,1)}), bf16[1,256,4,256]{1,3,0,2:T(8,128)(2,1)}, u32[]{:S(2)}, u32[]{:S(2)}) async-start(bf16[1,256,4,256]{1,3,0,2:T(8,128)(2,1)} %bitcast.265), calls=%async_computation.2 | async-start | bytes 1048576 | tf_op jit(solution)/shard_map/all_to_all | solution.py:185
  254.5 161.3 %reduce-scatter.8.cloned.1.call-start = ((), (), s32[]{:S(2)}) async-start(), calls=%async_computation.15 | async-start | bytes 4718592 | tf_op jit(solution)/shard_map/reduce_scatter | solution.py:218
  311.5 8.7 copy-start.17
  311.5 8.7 copy-start.19
  315.7 52.3 %all-to-all-start.3 = ((bf16[1,1024,3,1,256]{4,2,3,0,1:T(4,128)(2,1)}), bf16[1,1024,3,1,256]{4,2,3,0,1:T(4,128)(2,1)}, u32[]{:S(2)}, u32[]{:S(2)}) async-start(bf16[1,1024,3,1,256]{4,2,3,0,1:T(4,128)(2,1)} %copy.60), calls=%async_computation.3 | async-start | bytes 4194304 | tf_op jit(solution)/shard_map/all_to_all | solution.py:193
  320.1 114.7 %reduce-scatter.14.cloned.1.call-start = ((), (), s32[]{:S(2)}) async-start(), calls=%async_computation.18 | async-start | bytes 4718592 | tf_op jit(solution)/shard_map/reduce_scatter | solution.py:221
  370.9 4.6 copy-start.13
  376.0 5.6 copy-start.3
  382.8 2.5 copy-start.15
  385.2 145.6 %reduce-scatter.6.cloned.1.call-start = ((), (), s32[]{:S(2)}) async-start(), calls=%async_computation.14 | async-start | bytes 14155776 | tf_op jit(solution)/shard_map/reduce_scatter | solution.py:217
  394.1 256.3 %reduce-scatter.10.cloned.1.call-start = ((), (), s32[]{:S(2)}) async-start(), calls=%async_computation.16 | async-start | bytes 18874368 | tf_op jit(solution)/shard_map/reduce_scatter | solution.py:219
  404.2 365.5 %reduce-scatter.12.cloned.1.call-start = ((), (), s32[]{:S(2)}) async-start(), calls=%async_computation.17 | async-start | bytes 18874368 | tf_op jit(solution)/shard_map/reduce_scatter | solution.py:220
  415.5 488.7 %all-reduce.3.cloned.1.call-start = ((), (), s32[]{:S(2)}) async-start(), calls=%async_computation.19 | async-start | bytes 6815744 | tf_op jit(solution)/shard_map/psum | solution.py:224
  772.5 7.2 copy-start.5
  904.1 5.7 copy-start.10
  904.1 7.0 copy-start.12
  904.1 7.8 copy-start.11
  (3 other events, 3.6 us)
Sparse Core Ops, SparseCore 0:
  9.9 30.8 all-gather.5
  42.7 45.5 all-gather.7
  90.2 27.8 all-gather.9
  119.8 54.3 all-gather.11
  176.0 54.3 all-gather.13
  259.9 51.9 reduce-scatter.7
  385.3 49.4 reduce-scatter.13
  438.4 92.3 reduce-scatter.5
  534.4 115.9 reduce-scatter.9
  653.8 115.9 reduce-scatter.11
  773.1 130.9 all-reduce.2
where the time goes:
time: 925 us; the launch traced here: 920 us
  waiting for transfers between devices  626 us (68%)
  matrix products  133 us (14%)
  other arithmetic  50.3 us (5%)
  blocking collectives  42.3 us (5%)
  local copies, waits for them, and re-layouts  38.9 us (4%)
  between operations  15.2 us (2%)
  starting transfers between devices  13.1 us (1%)
    psum x1, waiting for transfers between devices, per_device(): lax.psum(first_sum[0].astype(jnp.bfloat16), 'seq').astype(jnp.float32)  123 us
    reduce_scatter x1, waiting for transfers between devices, per_device(): lax.psum_scatter(grad_up, 'dp', scatter_dimension=0, tiled=True)  117 us
    reduce_scatter x1, waiting for transfers between devices, per_device(): lax.psum_scatter(grad_down, 'dp', scatter_dimension=0, tiled=True)  117 us
    reduce_scatter x1, waiting for transfers between devices, per_device(): lax.psum_scatter(grad_qkv, 'dp', scatter_dimension=0, tiled=True)  94.2 us
    all_to_all x1, waiting for transfers between devices, per_device(): lax.all_to_all(grad_packed, 'seq', split_axis=1, concat_axis=3, tiled=True)  47.8 us
    all_gather x1, waiting for transfers between devices, per_device(): lax.all_gather(w_qkv, 'dp', axis=0, tiled=True)  44.9 us
    all_to_all x1, blocking collectives, per_device(): lax.all_to_all(packed, 'seq', split_axis=3, concat_axis=1, tiled=True)  42.3 us
    all_gather x1, waiting for transfers between devices, per_device(): lax.all_gather(w_time, 'dp', axis=1, tiled=True)  27.2 us
  transfers between devices with their start and end apart: 14, of which 11 were waited for; matrix products, arithmetic and copies ran while one was open for 21% of the time, Pallas kernels for 0%

commit v1 on v0

v1 whole, which is shorter than its diff:
```python
from functools import partial
import math

import jax
import jax.numpy as jnp
from jax import lax
from jax.sharding import PartitionSpec as P

HEAD_DIM = 64
TE = 256

highest = lax.Precision.HIGHEST
bf16 = jnp.bfloat16
f32 = jnp.float32


def normalize(values_in):
    centered = values_in - jnp.mean(values_in, axis=-1, keepdims=True)
    inverse = lax.rsqrt(jnp.mean(centered * centered, axis=-1, keepdims=True) + 1e-05)
    return (centered * inverse, inverse)


def norm_back(gradient, normed, inverse):
    return inverse * (
        gradient
        - jnp.mean(gradient, axis=-1, keepdims=True)
        - normed * jnp.mean(gradient * normed, axis=-1, keepdims=True)
    )


def time_embedding(noise_step):
    half_dim = TE // 2
    frequency = jnp.exp(-math.log(10000.0) * jnp.arange(half_dim, dtype=f32) / half_dim)
    angles = noise_step.astype(f32)[..., None] * frequency
    return jnp.concatenate([jnp.sin(angles), jnp.cos(angles)], axis=-1)


def rotate(values_in, positions, direction):
    half_dim = values_in.shape[-1] // 2
    frequency = jnp.exp(-math.log(10000.0) * jnp.arange(half_dim, dtype=f32) / half_dim)
    angles = positions[:, None, None] * frequency
    cosine = jnp.cos(angles)
    sine_wave = direction * jnp.sin(angles)
    first_half = values_in[..., :half_dim]
    second_half = values_in[..., half_dim:]
    return jnp.concatenate(
        [
            first_half * cosine - second_half * sine_wave,
            first_half * sine_wave + second_half * cosine,
        ],
        axis=-1,
    )


def hop(values_in, bit):
    count = lax.axis_size("dp")
    return lax.ppermute(values_in, "dp", [(i, i ^ bit) for i in range(count)])


def core_groups():
    count = lax.axis_size("dp")
    return [[i for i in range(count) if i % 2 == core] for core in range(2)]


def gather_chips(block):
    chips = lax.axis_size("dp") // 2
    if chips != 4:
        return lax.all_gather(block, "dp", axis=0, tiled=True, axis_index_groups=core_groups())
    rows = block.shape[0]
    half = rows // 2
    chip = lax.axis_index("dp") // 2
    from_x = hop(block, 2)
    from_y = hop(block, 4)
    far_top = hop(from_y[:half], 2)
    far_low = hop(from_x[half:], 4)
    out = jnp.zeros((chips * rows,) + block.shape[1:], block.dtype)
    for piece, other, shift in (
        (block, 0, 0),
        (from_x, 1, 0),
        (from_y, 2, 0),
        (far_top, 3, 0),
        (far_low, 3, half),
    ):
        out = lax.dynamic_update_slice_in_dim(out, piece, (chip ^ other) * rows + shift, axis=0)
    return out


def scatter_chips(parts):
    chips = lax.axis_size("dp") // 2
    if chips != 4:
        flat = parts.reshape((-1,) + parts.shape[2:])
        return lax.psum_scatter(
            flat, "dp", scatter_dimension=0, tiled=True, axis_index_groups=core_groups()
        ).astype(f32)
    half = parts.shape[1] // 2
    chip = lax.axis_index("dp") // 2
    own, to_x, to_y, to_far = [
        lax.dynamic_index_in_dim(parts, chip ^ other, 0, keepdims=False) for other in range(4)
    ]
    on_x = hop(to_far[:half], 2)
    on_y = hop(to_far[half:], 4)
    to_y = jnp.concatenate([to_y[:half] + on_x, to_y[half:]], axis=0)
    to_x = jnp.concatenate([to_x[:half], to_x[half:] + on_y], axis=0)
    return own.astype(f32) + hop(to_x, 2).astype(f32) + hop(to_y, 4).astype(f32)


def both_cores(half_block):
    chips = lax.axis_size("dp") // 2
    core = lax.axis_index("dp") % 2
    other = hop(half_block, 1)
    shape = (chips, half_block.shape[0] // chips) + half_block.shape[1:]
    mine, theirs = half_block.reshape(shape), other.reshape(shape)
    first = jnp.where(core == 0, mine, theirs)
    second = jnp.where(core == 0, theirs, mine)
    joined = jnp.stack([first, second], axis=1)
    return joined.reshape((-1,) + half_block.shape[1:])


def sum_cores(full):
    count = lax.axis_size("dp")
    core = lax.axis_index("dp") % 2
    view = full.reshape((count // 2, 2, full.shape[0] // count) + full.shape[1:])
    mine = lax.dynamic_index_in_dim(view, core, 1, keepdims=False)
    theirs = lax.dynamic_index_in_dim(view, 1 - core, 1, keepdims=False)
    return (mine.astype(f32) + hop(theirs.astype(bf16), 1).astype(f32)).astype(bf16)


def turn(values_in, step):
    count = lax.axis_size("seq")
    return lax.ppermute(values_in, "seq", [(i, (i + step) % count) for i in range(count)])


def shift(values_in, step):
    count = lax.axis_size("seq")
    return lax.ppermute(
        values_in, "seq", [(i, i + step) for i in range(count) if 0 <= i + step < count]
    )


def gather_seq(block):
    count = lax.axis_size("seq")
    place = lax.axis_index("seq")
    lower, upper = [block], [block]
    for _ in range(count - 1):
        lower.append(shift(lower[-1], 1))
        upper.append(shift(upper[-1], -1))
    return [block] + [
        jnp.where(place + step < count, upper[step], lower[count - step])
        for step in range(1, count)
    ]


def scatter_seq(blocks):
    count = len(blocks)
    right = left = None
    for step in range(1, count):
        going_right = blocks[count - step]
        going_left = blocks[step]
        if right is not None:
            going_right = going_right + right.astype(f32)
            going_left = going_left + left.astype(f32)
        right = shift(going_right.astype(bf16), 1)
        left = shift(going_left.astype(bf16), -1)
    return blocks[0] + right.astype(f32) + left.astype(f32)


def sum_seq(values_in):
    count = lax.axis_size("seq")
    if count != 4:
        return lax.psum(values_in.astype(bf16), "seq").astype(f32)
    place = lax.axis_index("seq")
    inner = lax.ppermute(values_in.astype(bf16), "seq", [(0, 1), (3, 2)])
    pair = values_in + inner.astype(f32)
    across = lax.ppermute(pair.astype(bf16), "seq", [(1, 2), (2, 1)])
    total = pair + across.astype(f32)
    outer = lax.ppermute(total.astype(bf16), "seq", [(1, 0), (2, 3)])
    return jnp.where((place == 0) | (place == 3), outer.astype(f32), total)


def attend_forward(queries, key_rows, values):
    scores = jnp.einsum("qhd,khd->hqk", queries, key_rows, preferred_element_type=f32) / math.sqrt(
        HEAD_DIM
    )
    row_top = jnp.max(scores, axis=-1, keepdims=True)
    exponent = jnp.exp(scores - row_top)
    row_total = jnp.sum(exponent, axis=-1, keepdims=True)
    probs = (exponent / row_total).astype(bf16)
    attended = jnp.einsum("hqk,khd->qhd", probs, values, preferred_element_type=f32)
    return attended.astype(bf16), (row_top + jnp.log(row_total))


def attend_backward(queries, key_rows, values, log_total, grad_attn):
    score_scale = 1.0 / math.sqrt(HEAD_DIM)
    scores = (
        jnp.einsum("qhd,khd->hqk", queries, key_rows, preferred_element_type=f32) * score_scale
    )
    probs = jnp.exp(scores - log_total)
    grad_probs = jnp.einsum("qhd,khd->hqk", grad_attn, values, preferred_element_type=f32)
    grad_scores = (
        probs * (grad_probs - jnp.sum(probs * grad_probs, axis=-1, keepdims=True))
    ).astype(bf16)
    grad_queries = (
        jnp.einsum("hqk,khd->qhd", grad_scores, key_rows, preferred_element_type=f32) * score_scale
    )
    grad_keys = (
        jnp.einsum("hqk,qhd->khd", grad_scores, queries, preferred_element_type=f32) * score_scale
    )
    grad_values = jnp.einsum(
        "hqk,qhd->khd", probs.astype(bf16), grad_attn, preferred_element_type=f32
    )
    return grad_queries.astype(bf16), grad_keys.astype(bf16), grad_values.astype(bf16)


def per_device(tokens, noise_steps, w_qkv, w_out, w_up, w_down, w_time, cotangent):
    dp_count, seq_parts = lax.axis_size("dp"), lax.axis_size("seq")
    chips = dp_count // 2
    core = lax.axis_index("dp") % 2
    place = lax.axis_index("seq")
    _, rows, width = tokens.shape
    group = width // seq_parts
    source = tokens[0]
    cot = cotangent[0]

    token_blocks = gather_seq(source)

    steps_all = lax.all_to_all(
        jnp.broadcast_to(noise_steps.astype(f32), (dp_count,)),
        "dp",
        split_axis=0,
        concat_axis=0,
        tiled=True,
    )
    embed_all = time_embedding(steps_all)
    cond_part = jnp.dot(embed_all, w_time.astype(f32), precision=highest)
    condition = lax.all_to_all(cond_part, "dp", split_axis=0, concat_axis=0, tiled=True).reshape(
        4, width
    )
    scale_a, shift_a, scale_b, shift_b = [condition[i][None, :] for i in range(4)]

    qkv_cols = lax.dynamic_index_in_dim(
        w_qkv.reshape(-1, 3, seq_parts, group), place, 2, keepdims=False
    ).reshape(-1, 3 * group)
    qkv_all = both_cores(gather_chips(qkv_cols))
    unit_view = w_up.reshape(w_up.shape[0], chips, 2, -1)
    up_mine = lax.dynamic_index_in_dim(unit_view, core, 2, keepdims=False).reshape(
        w_up.shape[0], -1
    )
    up_theirs = lax.dynamic_index_in_dim(unit_view, 1 - core, 2, keepdims=False).reshape(
        w_up.shape[0], -1
    )
    up_other = hop(up_theirs, 1)
    up_block = jnp.where(
        core == 0,
        jnp.concatenate([up_mine, up_other], axis=0),
        jnp.concatenate([up_other, up_mine], axis=0),
    )
    up_all = gather_chips(up_block)
    out_all = both_cores(gather_chips(w_out))
    down_all = gather_chips(w_down)
    cot_both = jnp.concatenate([cot, hop(cot, 1)], axis=0)

    full = jnp.concatenate(token_blocks, axis=0).astype(f32)
    normed_a, inverse_a = normalize(full)
    input_a = (normed_a * (1.0 + scale_a) + shift_a).astype(bf16)
    projected = jnp.dot(input_a, qkv_all, preferred_element_type=f32)
    block_place = (place + jnp.arange(seq_parts)) % seq_parts
    positions = (block_place[:, None] * rows + jnp.arange(rows)).reshape(-1).astype(f32)
    head_view = projected.reshape(seq_parts * rows, 3, -1, HEAD_DIM)
    queries = rotate(head_view[:, 0], positions, 1.0).astype(bf16)
    key_rows = rotate(head_view[:, 1], positions, 1.0).astype(bf16)
    values = head_view[:, 2].astype(bf16)
    attended, log_total = attend_forward(queries, key_rows, values)
    attended = attended.reshape(seq_parts, rows, group)
    pieces = [attended[0]] + [turn(attended[s], s) for s in range(1, seq_parts)]
    stacked = jnp.stack(pieces)
    mixed = jnp.concatenate(
        [
            lax.dynamic_index_in_dim(stacked, (place - g) % seq_parts, 0, keepdims=False)
            for g in range(seq_parts)
        ],
        axis=-1,
    )
    middle = source.astype(f32) + jnp.dot(mixed, out_all, preferred_element_type=f32)
    normed_b, inverse_b = normalize(middle)
    input_b = (normed_b * (1.0 + scale_b) + shift_b).astype(bf16)

    input_both = jnp.concatenate([input_b, hop(input_b, 1)], axis=0)
    upper = jnp.dot(input_both, up_all, preferred_element_type=f32)
    grad_hidden = lax.dot_general(
        cot_both, down_all, (((1,), (1,)), ((), ())), preferred_element_type=f32
    )
    hidden, gelu_pull = jax.vjp(partial(jax.nn.gelu, approximate=False), upper)
    hidden = hidden.astype(bf16)
    grad_upper = gelu_pull(grad_hidden)[0].astype(bf16)
    grad_in_part = lax.dot_general(
        grad_upper, up_all, (((1,), (1,)), ((), ())), preferred_element_type=f32
    )
    grad_in_b = grad_in_part[:rows] + hop(grad_in_part[rows:].astype(bf16), 1).astype(f32)
    out_part = jnp.dot(hidden, down_all, preferred_element_type=f32)
    result = (
        middle + out_part[:rows] + hop(out_part[rows:].astype(bf16), 1).astype(f32)
    ).astype(bf16)

    grad_down_part = lax.dot_general(
        hidden, cot_both, (((0,), (0,)), ((), ())), preferred_element_type=f32
    ).astype(bf16)
    grad_up_part = lax.dot_general(
        input_both, grad_upper, (((0,), (0,)), ((), ())), preferred_element_type=f32
    ).astype(bf16)

    grad_scale_b = jnp.sum(grad_in_b * normed_b, axis=0)
    grad_shift_b = jnp.sum(grad_in_b, axis=0)
    grad_middle = cot.astype(f32) + norm_back(grad_in_b * (1.0 + scale_b), normed_b, inverse_b)
    grad_branch = grad_middle.astype(bf16)
    grad_mixed = lax.dot_general(
        grad_branch, out_all, (((1,), (1,)), ((), ())), preferred_element_type=f32
    ).astype(bf16)
    to_heads = grad_mixed.reshape(rows, seq_parts, group)
    grad_pieces = [
        lax.dynamic_index_in_dim(to_heads, (place - s) % seq_parts, 1, keepdims=False)
        for s in range(seq_parts)
    ]
    grad_attn = jnp.concatenate(
        [grad_pieces[0]] + [turn(grad_pieces[s], -s) for s in range(1, seq_parts)], axis=0
    )
    grad_proj_part = lax.dot_general(
        mixed, grad_branch, (((0,), (0,)), ((), ())), preferred_element_type=f32
    )
    grad_q, grad_k, grad_v = attend_backward(
        queries,
        key_rows,
        values,
        log_total,
        grad_attn.reshape(seq_parts * rows, -1, HEAD_DIM),
    )
    grad_q = rotate(grad_q.astype(f32), positions, -1.0).astype(bf16)
    grad_k = rotate(grad_k.astype(f32), positions, -1.0).astype(bf16)
    grad_projected = jnp.stack([grad_q, grad_k, grad_v], axis=1).reshape(seq_parts * rows, -1)
    grad_in_a_part = lax.dot_general(
        grad_projected, qkv_all, (((1,), (1,)), ((), ())), preferred_element_type=f32
    )
    grad_qkv_part = lax.dot_general(
        input_a, grad_projected, (((0,), (0,)), ((), ())), preferred_element_type=f32
    )
    grad_in_a = scatter_seq(
        [grad_in_a_part[s * rows : (s + 1) * rows] for s in range(seq_parts)]
    )
    grad_scale_a = jnp.sum(grad_in_a_part * normed_a, axis=0)
    grad_shift_a = jnp.sum(grad_in_a_part, axis=0)
    grad_tokens = grad_middle + norm_back(
        grad_in_a * (1.0 + scale_a), normed_a[:rows], inverse_a[:rows]
    )

    grad_down = sum_seq(scatter_chips(grad_down_part.reshape(chips, -1, width)))
    grad_up_rows = scatter_chips(grad_up_part.reshape(chips, -1, grad_up_part.shape[1]))
    up_halves = grad_up_rows.reshape(2, -1, grad_up_rows.shape[1])
    keep = lax.dynamic_index_in_dim(up_halves, core, 0, keepdims=False)
    give = lax.dynamic_index_in_dim(up_halves, 1 - core, 0, keepdims=False)
    keep = keep.reshape(keep.shape[0], chips, -1)
    take = hop(give.astype(bf16), 1).astype(f32).reshape(keep.shape)
    grad_up = sum_seq(
        jnp.stack([jnp.where(core == 0, keep, take), jnp.where(core == 0, take, keep)], axis=2)
        .reshape(keep.shape[0], -1)
    )
    grad_proj = sum_seq(scatter_chips(sum_cores(grad_proj_part)))
    grad_qkv_cols = scatter_chips(sum_cores(grad_qkv_part)).astype(bf16)
    qkv_ring = jnp.stack(gather_seq(grad_qkv_cols))
    grad_qkv = jnp.stack(
        [
            lax.dynamic_index_in_dim(qkv_ring, (g - place) % seq_parts, 0, keepdims=False).reshape(
                -1, 3, group
            )
            for g in range(seq_parts)
        ],
        axis=2,
    )
    grad_qkv = grad_qkv.reshape(-1, 3 * width).astype(f32)
    grad_condition = jnp.concatenate([grad_scale_a, grad_shift_a, grad_scale_b, grad_shift_b])
    cond_cols = lax.all_to_all(
        grad_condition.reshape(dp_count, -1), "dp", split_axis=0, concat_axis=0, tiled=True
    )
    cond_sum = cond_cols
    for s in range(1, seq_parts):
        cond_sum = cond_sum + turn(cond_cols, s)
    grad_time = jnp.dot(embed_all.T, cond_sum, precision=highest)
    return (result[None], grad_tokens[None], grad_qkv, grad_proj, grad_up, grad_down, grad_time)


def solution(mesh):
    in_specs = (
        P("dp", "seq", None),
        P("dp"),
        P("dp", None),
        P("dp", None),
        P("dp", None),
        P("dp", None),
        P(None, "dp"),
        P("dp", "seq", None),
    )
    out_specs = (
        P("dp", "seq", None),
        P("dp", "seq", None),
        P("dp", None),
        P("dp", None),
        P("dp", None),
        P("dp", None),
        P(None, "dp"),
    )
    return jax.shard_map(
        per_device, mesh=mesh, in_specs=in_specs, out_specs=out_specs, check_vma=False
    )
```

time: 925 us -> 609 us (0.66)
  waiting for transfers between devices: 626 us -> 205 us
  starting transfers between devices: 13.1 us -> 119 us
  local copies, waits for them, and re-layouts: 38.9 us -> 90.9 us
  matrix products: 133 us -> 84.3 us
  other arithmetic: 50.3 us -> 98.1 us
  blocking collectives: 42.3 us -> 0 us
  between operations: 15.2 us -> 3.96 us
    reduce_scatter x5 -> x0, waiting for transfers between devices: 345 us -> none  [the longest x1 117 us: per_device(): lax.psum_scatter(grad_up, 'dp', scatter_dimension=0, tiled=True)]
    ppermute x0 -> x78, waiting for transfers between devices: none -> 193 us  [the longest x18 75.2 us: shift(): lax.ppermute(values_in, 'seq', [(i, i + step) for i in range(count) if 0...]
    psum x1 -> x0, waiting for transfers between devices: 123 us -> none  [per_device(): lax.psum(first_sum[0].astype(jnp.bfloat16), 'seq').astype(jnp.float32)]
    ppermute x0 -> x78, starting transfers between devices: none -> 108 us  [the longest x18 42.3 us: shift(): lax.ppermute(values_in, 'seq', [(i, i + step) for i in range(count) if 0...]
    all_gather x5 -> x0, waiting for transfers between devices: 83.2 us -> none  [the longest x1 44.9 us: per_device(): lax.all_gather(w_qkv, 'dp', axis=0, tiled=True)]
    all_to_all x3, waiting for transfers between devices: 71.6 us -> 11.6 us  [the longest x1 7.95 us: per_device(): lax.all_to_all(cond_part, 'dp', split_axis=0, concat_axis=0, tiled=True)]
    dot_general x35 -> x20, matrix products: 133 us -> 84.3 us  [the longest x1 13.1 us: attend_backward(): jnp.einsum('qhd,khd->hqk', grad_attn, values, preferred_element_type=f32)]
    all_to_all x1 -> x0, blocking collectives: 42.3 us -> none  [per_device(): lax.all_to_all(packed, 'seq', split_axis=3, concat_axis=1, tiled=True)]
  transfers between devices with their start and end apart: 14 -> 81, of which waited for: 11 -> 25; matrix products, arithmetic and copies ran while one was open for 21% -> 42% of each run, Pallas kernels for 0% -> 0%
where the time goes in v1:
time: 609 us; the launch traced here: 601 us
  waiting for transfers between devices  205 us (34%)
  starting transfers between devices  119 us (20%)
  other arithmetic  98.1 us (16%)
  local copies, waits for them, and re-layouts  90.9 us (15%)
  matrix products  84.3 us (14%)
    ppermute x18, waiting for transfers between devices, shift(): lax.ppermute(values_in, 'seq', [(i, i + step) for i in range(count) if 0...  75.2 us
    ppermute x42, waiting for transfers between devices, hop(): return lax.ppermute(values_in, 'dp', [(i, i ^ bit) for i in range(count)])  61.8 us
    ppermute x3, waiting for transfers between devices, sum_seq(): outer = lax.ppermute(total.astype(bf16), 'seq', [(1, 0), (2, 3)])  54.5 us
    ppermute x18, starting transfers between devices, shift(): lax.ppermute(values_in, 'seq', [(i, i + step) for i in range(count) if 0...  42.3 us
    ppermute x42, starting transfers between devices, hop(): return lax.ppermute(values_in, 'dp', [(i, i ^ bit) for i in range(count)])  35.7 us
    dynamic_update_slice x19, local copies, waits for them, and re-layouts, gather_chips(): lax.dynamic_update_slice_in_dim(out, piece, (chip ^ other) * rows + shift...  19.8 us
    unnamed x200, local copies, waits for them, and re-layouts  13.9 us
    dot_general x1, matrix products, attend_backward(): jnp.einsum('qhd,khd->hqk', grad_attn, values, preferred_element_type=f32)  13.1 us
  transfers between devices with their start and end apart: 81, of which 25 were waited for; matrix products, arithmetic and copies ran while one was open for 42% of the time, Pallas kernels for 0%

profile of v1, /device:TPU:0, one launch (start us, length us, event | category | flops | bytes accessed | tf_op | source)
XLA Modules:
  0.0 601.0 jit_solution(912409944372529028)
XLA Ops:
  8.7 4.2 all-to-all-start
  30.9 7.9 %all-to-all-done.1 = f32[8,1,512]{2,1,0:T(1,128)S(1)} async-done(((f32[8,1,512]{2,1,0:T(1,128)}), f32[8,1,512]{2,1,0:T(1,128)S(1)}, u32[]{:S(2)}, u32[]{:S(2)}) %all-to-all-start.1) | async-done | bytes 16416 | tf_op jit(solution)/shard_map/all_to_all | solution.py:235
  48.1 21.9 %collective-permute-done.8 = bf16[64,768]{0,1:T(8,128)(2,1)S(1)} collective-permute-done((bf16[64,768]{0,1:T(8,128)(2,1)}, bf16[64,768]{0,1:T(8,128)(2,1)S(1)}, u32[]{:S(2)}, u32[]{:S(2)}) %collective-permute-start.8) | collective-permute-done | bytes 98336 | tf_op jit(solution)/shard_map/ppermute | solution.py:57
  87.8 4.2 collective-permute-done
  92.0 4.2 collective-permute-start.2
  113.9 4.2 collective-permute-start.3
  123.7 5.0 collective-permute-done.3
  129.3 6.5 %collective-permute-done.5 = bf16[256,1024]{1,0:T(8,128)(2,1)S(1)} collective-permute-done((bf16[256,1024]{1,0:T(8,128)(2,1)}, bf16[256,1024]{1,0:T(8,128)(2,1)S(1)}, u32[]{:S(2)}, u32[]{:S(2)}) %collective-permute-start.5) | collective-permute-done | bytes 524320 | tf_op jit(solution)/shard_map/ppermute | solution.py:135
  142.6 7.2 %multiply_reduce_fusion.1 = (f32[4,1024]{1,0:T(4,128)S(1)}, f32[4,1024,1024]{1,2,0:T(8,128)}) fusion(bf16[1024,4,32]{0,2,1:T(8,128)(2,1)S(1)} %get-tuple-element.109, bf16[1024,4,32]{0,2,1:T(8,128)(2,1)S(1)} %get-tuple-element.110, bf16[1024,4,32]{0,2,1:T(8,128)(2,1)S(1)} %get-tuple-element.72, bf16[1024,4,32]{0,2,1:T(8,128)(2,1)S(1)} %get-tuple-element.71), kind=kOutput, calls=%fused_computation.6 | convolution fusion | flops 547352576 | bytes 17842176 | tf_op jit(solution)/shard_map/qhd,khd->hqk/dot_general | solution.py:181
  149.8 8.5 %fusion = f32[4,1024]{1,0:T(4,128)S(1)} fusion(f32[4,1024,1024]{1,2,0:T(8,128)} %get-tuple-element.121, f32[4,1024]{1,0:T(4,128)S(1)} %get-tuple-element.120), kind=kLoop, calls=%fused_computation.5 | loop fusion | flops 12578816 | bytes 16809984 | tf_op jit(solution)/shard_map/reduce_sum | solution.py:186
  158.3 9.7 %fusion.35 = bf16[1024,4,64]{0,2,1:T(8,128)(2,1)S(1)} fusion(f32[4,1024,1024]{1,2,0:T(8,128)} %get-tuple-element.121, f32[4,1024]{1,0:T(4,128)S(1)} %fusion, f32[4,1024]{1,0:T(4,128)S(1)} %get-tuple-element.120, f32[1024,3,4,64]{0,3,2,1:T(8,128)} %copy-done.23), kind=kOutput, calls=%fused_computation.76 | convolution fusion | flops 553910272 | bytes 17858560 | tf_op jit(solution)/shard_map/hqk,khd->qhd/dot_general | solution.py:188
  183.3 7.9 %collective-permute-done.28 = bf16[256,1024]{1,0:T(8,128)(2,1)S(1)} collective-permute-done((bf16[256,1024]{1,0:T(8,128)(2,1)S(1)}, bf16[256,1024]{1,0:T(8,128)(2,1)S(1)}, u32[]{:S(2)}, u32[]{:S(2)}) %collective-permute-start.28) | collective-permute-done | bytes 524320 | tf_op jit(solution)/shard_map/ppermute | solution.py:57
  193.4 6.1 %collective-permute-done.24 = bf16[128,2048]{0,1:T(8,128)(2,1)S(1)} collective-permute-done((bf16[128,2048]{0,1:T(8,128)(2,1)S(1)}, bf16[128,2048]{0,1:T(8,128)(2,1)S(1)}, u32[]{:S(2)}, u32[]{:S(2)}) %collective-permute-start.24) | collective-permute-done | bytes 524320 | tf_op jit(solution)/shard_map/ppermute | solution.py:57
  199.7 11.1 %multiply_convert_fusion.1 = (bf16[512,2048]{1,0:T(8,128)(2,1)S(1)}, f32[512,2048]{1,0:T(8,128)S(1)}, f32[512,2048]{1,0:T(8,128)S(1)}) fusion(bf16[1024,2048]{0,1:T(8,128)(2,1)S(1)} %constant_dynamic-update-slice_fusion.5, bf16[256,1024]{1,0:T(8,128)(2,1)S(1)} %collective-permute-done.19, bf16[256,1024]{1,0:T(8,128)(2,1)S(1)} %add_convert_fusion.6), kind=kOutput, calls=%fused_computation.19 | convolution fusion | flops 2217738240 | bytes 15728640 | tf_op jit(solution)/shard_map/dot_general | solution.py:288
  210.8 6.1 %add_convert_fusion = bf16[512,2048]{1,0:T(8,128)(2,1)S(1)} fusion(f32[512,2048]{1,0:T(8,128)S(1)} %get-tuple-element.38, f32[512,2048]{1,0:T(8,128)S(1)} %get-tuple-element.124, bf16[2048,1024]{1,0:T(8,128)(2,1)} %constant_dynamic-update-slice_fusion, bf16[256,1024]{1,0:T(8,128)(2,1)} %collective-permute-done.30, bf16[256,1024]{1,0:T(8,128)(2,1)} %bitcast.38), kind=kOutput, calls=%fused_computation.18 | convolution fusion | flops 2164260864 | bytes 15728640 | tf_op jit(solution)/shard_map/dot_general | solution.py:289
  219.3 4.6 fusion.105
  249.0 6.0 %collective-permute-done.60 = bf16[128,2048]{1,0:T(8,128)(2,1)} collective-permute-done((bf16[128,2048]{1,0:T(8,128)(2,1)}, bf16[128,2048]{1,0:T(8,128)(2,1)}, u32[]{:S(2)}, u32[]{:S(2)}) %collective-permute-start.60) | collective-permute-done | bytes 524320 | tf_op jit(solution)/shard_map/ppermute | solution.py:57
  271.9 7.7 %fusion.32 = bf16[1024,1,4,64]{0,3,2,1:T(8,128)(2,1)S(1)} fusion(f32[4,1024,1024]{1,2,0:T(8,128)} %get-tuple-element.121, f32[4,1024]{1,0:T(4,128)S(1)} %log_add_fusion, bf16[256,4,64]{0,2,1:T(8,128)(2,1)S(1)} %bitcast.289, bf16[256,4,64]{0,2,1:T(8,128)(2,1)S(1)} %bitcast.293, bf16[256,4,64]{0,2,1:T(8,128)(2,1)S(1)} %bitcast.291, ...), kind=kOutput, calls=%fused_computation.75 | convolution fusion | flops 551813120 | bytes 17842176 | tf_op jit(solution)/shard_map/hqk,qhd->khd/dot_general | solution.py:208
  279.6 13.1 %multiply_reduce_fusion = (f32[4,1024]{1,0:T(4,128)S(1)}, f32[4,1024,1024]{1,2,0:T(8,128)}) fusion(f32[4,1024,1024]{1,2,0:T(8,128)} %get-tuple-element.121, f32[4,1024]{1,0:T(4,128)S(1)} %log_add_fusion, f32[1024,3,4,64]{0,3,2,1:T(8,128)} %copy-done.23, bf16[256,4,64]{0,2,1:T(8,128)(2,1)S(1)} %bitcast.290, bf16[256,4,64]{0,2,1:T(8,128)(2,1)S(1)} %bitcast.294, ...), kind=kOutput, calls=%fused_computation.1 | convolution fusion | flops 555741184 | bytes 34635776 | tf_op jit(solution)/shard_map/qhd,khd->hqk/dot_general | solution.py:198
  292.8 7.9 %multiply_convert_fusion = bf16[4,1024,1024]{1,2,0:T(8,128)(2,1)S(1)} fusion(f32[4,1024,1024]{1,2,0:T(8,128)} %get-tuple-element.126, f32[4,1024,1024]{1,2,0:T(8,128)S(1)} %bitcast.251, f32[4,1024]{1,0:T(4,128)S(1)} %get-tuple-element.125, f32[4,1024]{1,0:T(4,128)S(1)} %log_add_fusion), kind=kLoop, calls=%fused_computation | loop fusion | flops 20971520 | bytes 41975808 | tf_op jit(solution)/shard_map/convert_element_type | solution.py:201
  345.1 7.3 %collective-permute-done.35 = bf16[256,1024]{1,0:T(8,128)(2,1)S(1)} collective-permute-done((bf16[256,1024]{1,0:T(8,128)(2,1)S(1)}, bf16[256,1024]{1,0:T(8,128)(2,1)S(1)}, u32[]{:S(2)}, u32[]{:S(2)}) %collective-permute-start.35) | collective-permute-done | bytes 524320 | tf_op jit(solution)/shard_map/ppermute | solution.py:135
  356.6 7.6 %collective-permute-done.44 = bf16[64,768]{1,0:T(8,128)(2,1)S(1)} collective-permute-done((bf16[64,768]{1,0:T(8,128)(2,1)S(1)}, bf16[64,768]{1,0:T(8,128)(2,1)S(1)}, u32[]{:S(2)}, u32[]{:S(2)}) %collective-permute-start.44) | collective-permute-done | bytes 98336 | tf_op jit(solution)/shard_map/ppermute | solution.py:57
  369.0 5.4 collective-permute-start.36
  378.0 4.1 collective-permute-done.71
  382.7 4.6 collective-permute-done.69
  414.3 29.8 %collective-permute-done.47 = bf16[128,768]{1,0:T(8,128)(2,1)} collective-permute-done((bf16[128,768]{1,0:T(8,128)(2,1)S(1)}, bf16[128,768]{1,0:T(8,128)(2,1)}, u32[]{:S(2)}, u32[]{:S(2)}) %collective-permute-start.47) | collective-permute-done | bytes 196640 | tf_op jit(solution)/shard_map/ppermute | solution.py:135
  445.5 5.8 collective-permute-start.48
  464.9 4.6 collective-permute-start.57
  479.7 21.1 %collective-permute-done.49 = bf16[128,768]{1,0:T(8,128)(2,1)S(1)} collective-permute-done((bf16[128,768]{1,0:T(8,128)(2,1)}, bf16[128,768]{1,0:T(8,128)(2,1)S(1)}, u32[]{:S(2)}, u32[]{:S(2)}) %collective-permute-start.49) | collective-permute-done | bytes 196640 | tf_op jit(solution)/shard_map/ppermute | solution.py:135
  537.2 4.7 collective-permute-done.59
  543.9 32.2 %collective-permute-done.74 = bf16[512,1024]{1,0:T(8,128)(2,1)S(1)} collective-permute-done((bf16[512,1024]{1,0:T(8,128)(2,1)S(1)}, bf16[512,1024]{1,0:T(8,128)(2,1)S(1)}, u32[]{:S(2)}, u32[]{:S(2)}) %collective-permute-start.74) | collective-permute-done | bytes 1048608 | tf_op jit(solution)/shard_map/ppermute | solution.py:176
  580.1 17.6 %collective-permute-done.67 = bf16[128,4096]{1,0:T(8,128)(2,1)S(1)} collective-permute-done((bf16[128,4096]{1,0:T(8,128)(2,1)S(1)}, bf16[128,4096]{1,0:T(8,128)(2,1)S(1)}, u32[]{:S(2)}, u32[]{:S(2)}) %collective-permute-start.67) | collective-permute-done | bytes 1048608 | tf_op jit(solution)/shard_map/ppermute | solution.py:176
  (507 shorter events, 298.4 us)
Async XLA Ops:
  0.7 42.2 %collective-permute-start.15 = (bf16[128,1024]{1,0:T(8,128)(2,1)}, bf16[128,1024]{1,0:T(8,128)(2,1)}, u32[]{:S(2)}, u32[]{:S(2)}) collective-permute-start(bf16[128,1024]{1,0:T(8,128)(2,1)} %param.11), channel_id=1, source_target_pairs={{0,16},{4,20},{8,24},{12,28},{16,0},{20,4},{24,8},{28,12},{1,17},{... | collective-permute-start | bytes 786440 | tf_op jit(solution)/shard_map/ppermute | solution.py:57
  3.7 41.8 %collective-permute-start.14 = (bf16[128,1024]{1,0:T(8,128)(2,1)}, bf16[128,1024]{1,0:T(8,128)(2,1)}, u32[]{:S(2)}, u32[]{:S(2)}) collective-permute-start(bf16[128,1024]{1,0:T(8,128)(2,1)} %param.11), channel_id=1, source_target_pairs={{0,8},{4,12},{8,0},{12,4},{16,24},{20,28},{24,16},{28,20},{1,9},{5... | collective-permute-start | bytes 786440 | tf_op jit(solution)/shard_map/ppermute | solution.py:57
  6.7 32.7 %collective-permute-start.7 = (bf16[128,768]{0,1:T(8,128)(2,1)S(1)}, bf16[128,768]{0,1:T(8,128)(2,1)}, u32[]{:S(2)}, u32[]{:S(2)}) collective-permute-start(bf16[128,768]{0,1:T(8,128)(2,1)S(1)} %bitcast.299), channel_id=1, source_target_pairs={{0,16},{4,20},{8,24},{12,28},{16,0},{20,4},{24,8},{28,12},{1,17},{... | collective-permute-start | bytes 589832 | tf_op jit(solution)/shard_map/ppermute | solution.py:57
  7.3 35.0 %collective-permute-start.6 = (bf16[128,768]{0,1:T(8,128)(2,1)S(1)}, bf16[128,768]{0,1:T(8,128)(2,1)S(1)}, u32[]{:S(2)}, u32[]{:S(2)}) collective-permute-start(bf16[128,768]{0,1:T(8,128)(2,1)S(1)} %bitcast.300), channel_id=1, source_target_pairs={{0,8},{4,12},{8,0},{12,4},{16,24},{20,28},{24,16},{28,20},{1,9},{5... | collective-permute-start | bytes 589832 | tf_op jit(solution)/shard_map/ppermute | solution.py:57
  12.8 83.4 %collective-permute-start.26 = (bf16[512,1024]{1,0:T(8,128)(2,1)}, bf16[512,1024]{1,0:T(8,128)(2,1)}, u32[]{:S(2)}, u32[]{:S(2)}) collective-permute-start(bf16[512,1024]{1,0:T(8,128)(2,1)} %param.13), channel_id=1, source_target_pairs={{0,16},{4,20},{8,24},{12,28},{16,0},{20,4},{24,8},{28,12},{1,17},{... | collective-permute-start | bytes 3145736 | tf_op jit(solution)/shard_map/ppermute | solution.py:57
  39.5 63.3 %collective-permute-start.25 = (bf16[512,1024]{1,0:T(8,128)(2,1)}, bf16[512,1024]{1,0:T(8,128)(2,1)}, u32[]{:S(2)}, u32[]{:S(2)}) collective-permute-start(bf16[512,1024]{1,0:T(8,128)(2,1)} %param.13), channel_id=1, source_target_pairs={{0,8},{4,12},{8,0},{12,4},{16,24},{20,28},{24,16},{28,20},{1,9},{5... | collective-permute-start | bytes 3145736 | tf_op jit(solution)/shard_map/ppermute | solution.py:57
  42.3 27.7 %collective-permute-start.8 = (bf16[64,768]{0,1:T(8,128)(2,1)}, bf16[64,768]{0,1:T(8,128)(2,1)S(1)}, u32[]{:S(2)}, u32[]{:S(2)}) collective-permute-start(bf16[64,768]{0,1:T(8,128)(2,1)} %bitcast.249), channel_id=1, source_target_pairs={{0,8},{4,12},{8,0},{12,4},{16,24},{20,28},{24,16},{28,20},{1,9},{5... | collective-permute-start | bytes 294920 | tf_op jit(solution)/shard_map/ppermute | solution.py:57
  43.8 35.4 %collective-permute-start.16 = (bf16[64,1024]{1,0:T(8,128)(2,1)S(1)}, bf16[64,1024]{1,0:T(8,128)(2,1)S(1)}, u32[]{:S(2)}, u32[]{:S(2)}) collective-permute-start(bf16[64,1024]{1,0:T(8,128)(2,1)S(1)} %slice.374), channel_id=1, source_target_pairs={{0,8},{4,12},{8,0},{12,4},{16,24},{20,28},{24,16},{28,20},{1,9},{5... | collective-permute-start | bytes 393224 | tf_op jit(solution)/shard_map/ppermute | solution.py:57
  46.4 34.1 %collective-permute-start.17 = (bf16[64,1024]{1,0:T(8,128)(2,1)S(1)}, bf16[64,1024]{1,0:T(8,128)(2,1)S(1)}, u32[]{:S(2)}, u32[]{:S(2)}) collective-permute-start(bf16[64,1024]{1,0:T(8,128)(2,1)S(1)} %slice.375), channel_id=1, source_target_pairs={{0,16},{4,20},{8,24},{12,28},{16,0},{20,4},{24,8},{28,12},{1,17},{... | collective-permute-start | bytes 393224 | tf_op jit(solution)/shard_map/ppermute | solution.py:57
  91.9 28.3 %collective-permute-start.18 = (bf16[512,1024]{1,0:T(8,128)(2,1)}, bf16[512,1024]{1,0:T(8,128)(2,1)}, u32[]{:S(2)}, u32[]{:S(2)}) collective-permute-start(bf16[512,1024]{1,0:T(8,128)(2,1)} %constant_dynamic-update-slice_fusion.10), channel_id=1, source_target_pairs={{0,4},{4,0},{8,12},{12,8},{16,20},{20,16},{24,28},{28,24},{1,5},{5... | collective-permute-start | bytes 3145736 | tf_op jit(solution)/shard_map/ppermute | solution.py:57
  102.8 108.0 %collective-permute-start.30 = (bf16[256,1024]{1,0:T(8,128)(2,1)}, bf16[256,1024]{1,0:T(8,128)(2,1)}, u32[]{:S(2)}, u32[]{:S(2)}) collective-permute-start(bf16[256,1024]{1,0:T(8,128)(2,1)} %bitcast.38), channel_id=1, source_target_pairs={{0,4},{4,0},{8,12},{12,8},{16,20},{20,16},{24,28},{28,24},{1,5},{5... | collective-permute-start | bytes 1572872 | tf_op jit(solution)/shard_map/ppermute | solution.py:57
  109.6 58.5 %collective-permute-start.21 = (bf16[256,2048]{0,1:T(8,128)(2,1)}, bf16[256,2048]{0,1:T(8,128)(2,1)}, u32[]{:S(2)}, u32[]{:S(2)}) collective-permute-start(bf16[256,2048]{0,1:T(8,128)(2,1)} %get-tuple-element.40), channel_id=1, source_target_pairs={{0,8},{4,12},{8,0},{12,4},{16,24},{20,28},{24,16},{28,20},{1,9},{5... | collective-permute-start | bytes 3145736 | tf_op jit(solution)/shard_map/ppermute | solution.py:57
  112.1 59.8 %collective-permute-start.22 = (bf16[256,2048]{0,1:T(8,128)(2,1)}, bf16[256,2048]{0,1:T(8,128)(2,1)}, u32[]{:S(2)}, u32[]{:S(2)}) collective-permute-start(bf16[256,2048]{0,1:T(8,128)(2,1)} %get-tuple-element.40), channel_id=1, source_target_pairs={{0,16},{4,20},{8,24},{12,28},{16,0},{20,4},{24,8},{28,12},{1,17},{... | collective-permute-start | bytes 3145736 | tf_op jit(solution)/shard_map/ppermute | solution.py:57
  128.8 47.5 %collective-permute-start.27 = (bf16[256,1024]{1,0:T(8,128)(2,1)}, bf16[256,1024]{1,0:T(8,128)(2,1)}, u32[]{:S(2)}, u32[]{:S(2)}) collective-permute-start(bf16[256,1024]{1,0:T(8,128)(2,1)} %slice.380), channel_id=1, source_target_pairs={{0,8},{4,12},{8,0},{12,4},{16,24},{20,28},{24,16},{28,20},{1,9},{5... | collective-permute-start | bytes 1572872 | tf_op jit(solution)/shard_map/ppermute | solution.py:57
  229.6 33.7 %collective-permute-start.68 = (bf16[256,1024]{1,0:T(8,128)(2,1)}, bf16[256,1024]{1,0:T(8,128)(2,1)}, u32[]{:S(2)}, u32[]{:S(2)}) collective-permute-start(bf16[256,1024]{1,0:T(8,128)(2,1)} %get-tuple-element.42), channel_id=1, source_target_pairs={{0,16},{4,20},{8,24},{12,28},{16,0},{20,4},{24,8},{28,12},{1,17},{... | collective-permute-start | bytes 1572872 | tf_op jit(solution)/shard_map/ppermute | solution.py:57
  230.1 33.8 %collective-permute-start.70 = (bf16[256,1024]{1,0:T(8,128)(2,1)}, bf16[256,1024]{1,0:T(8,128)(2,1)}, u32[]{:S(2)}, u32[]{:S(2)}) collective-permute-start(bf16[256,1024]{1,0:T(8,128)(2,1)} %get-tuple-element.44), channel_id=1, source_target_pairs={{0,8},{4,12},{8,0},{12,4},{16,24},{20,28},{24,16},{28,20},{1,9},{5... | collective-permute-start | bytes 1572872 | tf_op jit(solution)/shard_map/ppermute | solution.py:57
  263.3 105.7 %collective-permute-start.63 = (bf16[256,2048]{1,0:T(8,128)(2,1)}, bf16[256,2048]{1,0:T(8,128)(2,1)}, u32[]{:S(2)}, u32[]{:S(2)}) collective-permute-start(bf16[256,2048]{1,0:T(8,128)(2,1)} %pad_maximum_fusion.8), channel_id=1, source_target_pairs={{0,16},{4,20},{8,24},{12,28},{16,0},{20,4},{24,8},{28,12},{1,17},{... | collective-permute-start | bytes 3145736 | tf_op jit(solution)/shard_map/ppermute | solution.py:57
  338.0 36.4 %collective-permute-start.61 = (bf16[256,2048]{1,0:T(8,128)(2,1)S(1)}, bf16[256,2048]{1,0:T(8,128)(2,1)S(1)}, u32[]{:S(2)}, u32[]{:S(2)}) collective-permute-start(bf16[256,2048]{1,0:T(8,128)(2,1)S(1)} %copy-done.50), channel_id=1, source_target_pairs={{0,8},{4,12},{8,0},{12,4},{16,24},{20,28},{24,16},{28,20},{1,9},{5... | collective-permute-start | bytes 3145736 | tf_op jit(solution)/shard_map/ppermute | solution.py:57
  338.6 27.8 %collective-permute-start.52 = (bf16[4,128,1024]{2,1,0:T(8,128)(2,1)S(1)}, bf16[4,128,1024]{2,1,0:T(8,128)(2,1)S(1)}, u32[]{:S(2)}, u32[]{:S(2)}) collective-permute-start(bf16[4,128,1024]{2,1,0:T(8,128)(2,1)S(1)} %copy-done.49), channel_id=1, source_target_pairs={{0,4},{4,0},{8,12},{12,8},{16,20},{20,16},{24,28},{28,24},{1,5},{5... | collective-permute-start | bytes 3145736 | tf_op jit(solution)/shard_map/ppermute | solution.py:57
  366.5 31.8 %collective-permute-start.38 = (bf16[256,1024]{1,0:T(8,128)(2,1)}, bf16[256,1024]{1,0:T(8,128)(2,1)}, u32[]{:S(2)}, u32[]{:S(2)}) collective-permute-start(bf16[256,1024]{1,0:T(8,128)(2,1)} %get-tuple-element.56), channel_id=1, source_target_pairs={{1,0},{2,1},{3,2},{5,4},{6,5},{7,6},{9,8},{10,9},{11,10},{13,12},{... | collective-permute-start | bytes 1572872 | tf_op jit(solution)/shard_map/ppermute | solution.py:135
  369.0 30.4 %collective-permute-start.36 = (bf16[256,1024]{1,0:T(8,128)(2,1)}, bf16[256,1024]{1,0:T(8,128)(2,1)}, u32[]{:S(2)}, u32[]{:S(2)}) collective-permute-start(bf16[256,1024]{1,0:T(8,128)(2,1)} %add_convert_fusion.5), channel_id=1, source_target_pairs={{0,1},{1,2},{2,3},{4,5},{5,6},{6,7},{8,9},{9,10},{10,11},{12,13},{... | collective-permute-start | bytes 1572872 | tf_op jit(solution)/shard_map/ppermute | solution.py:135
  374.4 29.2 %collective-permute-start.45 = (bf16[128,768]{1,0:T(8,128)(2,1)}, bf16[128,768]{1,0:T(8,128)(2,1)}, u32[]{:S(2)}, u32[]{:S(2)}) collective-permute-start(bf16[128,768]{1,0:T(8,128)(2,1)} %pad_maximum_fusion.30), channel_id=1, source_target_pairs={{0,16},{4,20},{8,24},{12,28},{16,0},{20,4},{24,8},{28,12},{1,17},{... | collective-permute-start | bytes 589832 | tf_op jit(solution)/shard_map/ppermute | solution.py:57
  396.3 55.0 %collective-permute-start.64 = (bf16[128,2048]{1,0:T(8,128)(2,1)}, bf16[128,2048]{1,0:T(8,128)(2,1)S(1)}, u32[]{:S(2)}, u32[]{:S(2)}) collective-permute-start(bf16[128,2048]{1,0:T(8,128)(2,1)} %fusion.47), channel_id=1, source_target_pairs={{0,4},{4,0},{8,12},{12,8},{16,20},{20,16},{24,28},{28,24},{1,5},{5... | collective-permute-start | bytes 1572872 | tf_op jit(solution)/shard_map/ppermute | solution.py:57
  403.5 114.5 %collective-permute-start.72 = (bf16[512,1024]{1,0:T(8,128)(2,1)}, bf16[512,1024]{1,0:T(8,128)(2,1)}, u32[]{:S(2)}, u32[]{:S(2)}) collective-permute-start(bf16[512,1024]{1,0:T(8,128)(2,1)} %fusion.97), channel_id=1, source_target_pairs={{0,1},{3,2},{4,5},{7,6},{8,9},{11,10},{12,13},{15,14},{16,17},{19,... | collective-permute-start | bytes 3145736 | tf_op jit(solution)/shard_map/ppermute | solution.py:172
  407.0 119.9 %collective-permute-start.37 = (bf16[256,1024]{1,0:T(8,128)(2,1)}, bf16[256,1024]{1,0:T(8,128)(2,1)}, u32[]{:S(2)}, u32[]{:S(2)}) collective-permute-start(bf16[256,1024]{1,0:T(8,128)(2,1)} %get-tuple-element.53), channel_id=1, source_target_pairs={{0,1},{1,2},{2,3},{4,5},{5,6},{6,7},{8,9},{9,10},{10,11},{12,13},{... | collective-permute-start | bytes 1572872 | tf_op jit(solution)/shard_map/ppermute | solution.py:135
  410.2 34.0 %collective-permute-start.47 = (bf16[128,768]{1,0:T(8,128)(2,1)S(1)}, bf16[128,768]{1,0:T(8,128)(2,1)}, u32[]{:S(2)}, u32[]{:S(2)}) collective-permute-start(bf16[128,768]{1,0:T(8,128)(2,1)S(1)} %fusion.56), channel_id=1, source_target_pairs={{0,1},{1,2},{2,3},{4,5},{5,6},{6,7},{8,9},{9,10},{10,11},{12,13},{... | collective-permute-start | bytes 589832 | tf_op jit(solution)/shard_map/ppermute | solution.py:135
  412.2 33.3 %collective-permute-start.46 = (bf16[128,768]{1,0:T(8,128)(2,1)S(1)}, bf16[128,768]{1,0:T(8,128)(2,1)}, u32[]{:S(2)}, u32[]{:S(2)}) collective-permute-start(bf16[128,768]{1,0:T(8,128)(2,1)S(1)} %fusion.56), channel_id=1, source_target_pairs={{1,0},{2,1},{3,2},{5,4},{6,5},{7,6},{9,8},{10,9},{11,10},{13,12},{... | collective-permute-start | bytes 589832 | tf_op jit(solution)/shard_map/ppermute | solution.py:135
  444.2 28.5 %collective-permute-start.39 = (bf16[256,1024]{1,0:T(8,128)(2,1)}, bf16[256,1024]{1,0:T(8,128)(2,1)}, u32[]{:S(2)}, u32[]{:S(2)}) collective-permute-start(bf16[256,1024]{1,0:T(8,128)(2,1)} %get-tuple-element.54), channel_id=1, source_target_pairs={{1,0},{2,1},{3,2},{5,4},{6,5},{7,6},{9,8},{10,9},{11,10},{13,12},{... | collective-permute-start | bytes 1572872 | tf_op jit(solution)/shard_map/ppermute | solution.py:135
  469.5 52.4 %collective-permute-start.65 = (bf16[128,4096]{1,0:T(8,128)(2,1)}, bf16[128,4096]{1,0:T(8,128)(2,1)}, u32[]{:S(2)}, u32[]{:S(2)}) collective-permute-start(bf16[128,4096]{1,0:T(8,128)(2,1)} %convert_element_type.372), channel_id=1, source_target_pairs={{0,1},{3,2},{4,5},{7,6},{8,9},{11,10},{12,13},{15,14},{16,17},{19,... | collective-permute-start | bytes 3145736 | tf_op jit(solution)/shard_map/ppermute | solution.py:172
  472.7 28.0 %collective-permute-start.49 = (bf16[128,768]{1,0:T(8,128)(2,1)}, bf16[128,768]{1,0:T(8,128)(2,1)S(1)}, u32[]{:S(2)}, u32[]{:S(2)}) collective-permute-start(bf16[128,768]{1,0:T(8,128)(2,1)} %collective-permute-done.48), channel_id=1, source_target_pairs={{0,1},{1,2},{2,3},{4,5},{5,6},{6,7},{8,9},{9,10},{10,11},{12,13},{... | collective-permute-start | bytes 589832 | tf_op jit(solution)/shard_map/ppermute | solution.py:135
  531.3 44.8 %collective-permute-start.74 = (bf16[512,1024]{1,0:T(8,128)(2,1)S(1)}, bf16[512,1024]{1,0:T(8,128)(2,1)S(1)}, u32[]{:S(2)}, u32[]{:S(2)}) collective-permute-start(bf16[512,1024]{1,0:T(8,128)(2,1)S(1)} %fusion.42), channel_id=1, source_target_pairs={{1,0},{2,3},{5,4},{6,7},{9,8},{10,11},{13,12},{14,15},{17,16},{18,... | collective-permute-start | bytes 3145736 | tf_op jit(solution)/shard_map/ppermute | solution.py:176
  534.6 63.1 %collective-permute-start.67 = (bf16[128,4096]{1,0:T(8,128)(2,1)S(1)}, bf16[128,4096]{1,0:T(8,128)(2,1)S(1)}, u32[]{:S(2)}, u32[]{:S(2)}) collective-permute-start(bf16[128,4096]{1,0:T(8,128)(2,1)S(1)} %fusion.41), channel_id=1, source_target_pairs={{1,0},{2,3},{5,4},{6,7},{9,8},{10,11},{13,12},{14,15},{17,16},{18,... | collective-permute-start | bytes 3145736 | tf_op jit(solution)/shard_map/ppermute | solution.py:176
  (146 other events, 2293.7 us)

commit v2 on v1

--- a/solution.py
+++ b/solution.py
@@ -4,6 +4,8 @@
 import jax
 import jax.numpy as jnp
 from jax import lax
+from jax.experimental import pallas as pl
+from jax.experimental.pallas import tpu as pltpu
 from jax.sharding import PartitionSpec as P
 
 HEAD_DIM = 64
@@ -211,7 +213,7 @@
     return grad_queries.astype(bf16), grad_keys.astype(bf16), grad_values.astype(bf16)
 
 
-def per_device(tokens, noise_steps, w_qkv, w_out, w_up, w_down, w_time, cotangent):
+def per_device_any(tokens, noise_steps, w_qkv, w_out, w_up, w_down, w_time, cotangent):
     dp_count, seq_parts = lax.axis_size("dp"), lax.axis_size("seq")
     chips = dp_count // 2
     core = lax.axis_index("dp") % 2
@@ -386,6 +388,760 @@
     return (result[None], grad_tokens[None], grad_qkv, grad_proj, grad_up, grad_down, grad_time)
 
 
+NT = (((1,), (1,)), ((), ()))
+TN = (((0,), (0,)), ((), ()))
+VMEM = pl.BlockSpec(memory_space=pltpu.VMEM)
+SMEM = pl.BlockSpec(memory_space=pltpu.SMEM)
+LANES = 128
+
+
+def call(kernel, name, outs, me, *operands, scratch=(), flops=10**8, limit=40):
+    moved = sum(x.size * x.dtype.itemsize for x in operands)
+    return pl.pallas_call(
+        kernel,
+        name=name,
+        out_shape=[jax.ShapeDtypeStruct(shape, kind) for shape, kind in outs],
+        in_specs=[SMEM] + [VMEM] * len(operands),
+        out_specs=[VMEM] * len(outs),
+        scratch_shapes=list(scratch),
+        compiler_params=pltpu.CompilerParams(vmem_limit_bytes=limit * 2**20),
+        cost_estimate=pl.CostEstimate(flops=flops, bytes_accessed=moved, transcendentals=0),
+    )(me, *operands)
+
+
+def dot(left, right, dims=(((1,), (0,)), ((), ()))):
+    return lax.dot_general(left, right, dims, preferred_element_type=f32)
+
+
+def lanes(start, size):
+    return pl.ds(pl.multiple_of(start, LANES), size)
+
+
+def partner(values_in):
+    half = HEAD_DIM // 2
+    lane = lax.broadcasted_iota(jnp.int32, values_in.shape, 1)
+    return jnp.where(
+        lane % HEAD_DIM < half,
+        pltpu.roll(values_in, values_in.shape[1] - half, 1),
+        pltpu.roll(values_in, half, 1),
+    )
+
+
+def pack_kernel(me, w_qkv, w_out, w_up, first, up_keep, up_give):
+    core, place = me[1], me[2]
+    width = w_out.shape[1]
+    group = width // 4
+    for part in range(3):
+        first[:, part * group : (part + 1) * group] = w_qkv[
+            :, lanes(part * width + place * group, group)
+        ]
+    first[:, 3 * group :] = w_out[...]
+    units = w_up.shape[1] // 8
+    for chip in range(4):
+        at = slice(chip * units, (chip + 1) * units)
+        up_keep[:, at] = w_up[:, lanes((2 * chip + core) * units, units)]
+        up_give[:, at] = w_up[:, lanes((2 * chip + 1 - core) * units, units)]
+
+
+def pack_ffn_kernel(me, keep, take, w_down, out):
+    core = me[1]
+    rows, half = keep.shape[0], keep.shape[1] // 2
+    for j in range(2):
+        at = slice(j * half, (j + 1) * half)
+        out[lanes(2 * j * rows + core * rows, rows), :] = keep[:, at]
+        out[lanes(2 * j * rows + (1 - core) * rows, rows), :] = take[:, at]
+    out[4 * rows :, :] = w_down[...]
+
+
+def unpack_kernel(me, *refs):
+    qkv_all, out_all = refs[-2:]
+    chip, core = me[0], me[1]
+    rows = refs[0].shape[0]
+    cut = qkv_all.shape[1]
+    for side in range(2):
+        owner = core if side == 0 else 1 - core
+        own, on_x, on_y, top, low = refs[5 * side : 5 * side + 5]
+        for piece, other, start in (
+            (own, 0, 0),
+            (on_x, 1, 0),
+            (on_y, 2, 0),
+            (top, 3, 0),
+            (low, 3, rows // 2),
+        ):
+            at = pl.ds(
+                pl.multiple_of(((chip ^ other) * 2 + owner) * rows + start, rows // 2),
+                piece.shape[0],
+            )
+            qkv_all[at, :] = piece[:, :cut]
+            out_all[at, :] = piece[:, cut:]
+
+
+def qkv_kernel(me, *refs):
+    blocks = refs[:7]
+    scale, shift, weight, cosine, sine, normed, input_a, q_out, k_out, v_out = refs[7:]
+    place = me[2]
+    rows, group = blocks[0].shape[0], q_out.shape[1]
+    for s in range(4):
+        at = slice(s * rows, (s + 1) * rows)
+        block = blocks[0][...].astype(f32)
+        if s:
+            block = jnp.where(
+                place + s < 4, blocks[s][...].astype(f32), blocks[7 - s][...].astype(f32)
+            )
+        centred, _ = normalize(block)
+        normed[at, :] = centred
+        low = (centred * (1.0 + scale[...]) + shift[...]).astype(bf16)
+        input_a[at, :] = low
+        for part, out in enumerate((q_out, k_out, v_out)):
+            projected = dot(low, weight[:, part * group : (part + 1) * group])
+            if part == 2:
+                out[at, :] = projected.astype(bf16)
+                continue
+            for j in range(0, group, LANES):
+                piece = projected[:, j : j + LANES]
+                piece = piece * cosine[at, :] + partner(piece) * sine[at, :]
+                if part == 0:
+                    piece = piece * (1.0 / math.sqrt(HEAD_DIM))
+                out[at, j : j + LANES] = piece.astype(bf16)
+
+
+def attend_kernel(me, queries, keys, values, out, log_total):
+    count, group = queries.shape
+    step = 512
+    lane = lax.broadcasted_iota(jnp.int32, (step, LANES), 1)
+    for i in range(0, count, step):
+        at = slice(i, i + step)
+        stats = jnp.zeros((step, LANES), f32)
+        for j in range(group // LANES):
+            cols = slice(j * LANES, (j + 1) * LANES)
+            halves = []
+            for side in range(2):
+                query = jnp.where(
+                    lane // HEAD_DIM == side, queries[at, cols], jnp.zeros((), bf16)
+                )
+                scores = dot(query, keys[:, cols], NT)
+                top = jnp.max(scores, axis=1, keepdims=True)
+                exponent = jnp.exp(scores - top)
+                total = jnp.sum(exponent, axis=1, keepdims=True)
+                halves.append(dot(exponent.astype(bf16), values[:, cols]) / total)
+                stats = jnp.where(lane == 2 * j + side, top + jnp.log(total), stats)
+            out[at, cols] = jnp.where(lane < HEAD_DIM, halves[0], halves[1]).astype(bf16)
+        log_total[:, at] = jnp.transpose(stats)[:8]
+
+
+def attend_back_kernel(
+    me, queries, keys, values, g0, g1, g2, g3, log_total, cosine, sine, out, key_sum, value_sum, query_t
+):
+    count, group = queries.shape
+    step = 512
+    rows = g0.shape[0]
+    pieces = (g0, g1, g2, g3)
+    keys_t = jnp.transpose(keys[...])
+    lane = lax.broadcasted_iota(jnp.int32, (step, LANES), 1)
+    for j in range(group // LANES):
+        cols = slice(j * LANES, (j + 1) * LANES)
+        for i in range(0, count, step):
+            at = slice(i, i + step)
+            grad = jnp.concatenate(
+                [pieces[(i + n) // rows][:, cols] for n in range(0, step, rows)], axis=0
+            )
+            for side in range(2):
+                head = 2 * j + side
+                mine = slice(head * HEAD_DIM, (head + 1) * HEAD_DIM)
+                keep = lane // HEAD_DIM == side
+                query = jnp.where(keep, queries[at, cols], jnp.zeros((), bf16))
+                grad_mine = jnp.where(keep, grad, jnp.zeros((), bf16))
+                probs = jnp.exp(dot(keys[:, cols], query, NT) - log_total[head : head + 1, at])
+                grad_probs = dot(values[:, cols], grad_mine, NT)
+                delta = jnp.sum(probs * grad_probs, axis=0, keepdims=True)
+                grad_scores = (probs * (grad_probs - delta)).astype(bf16)
+                value_part = dot(probs.astype(bf16), grad_mine)
+                key_part = dot(grad_scores, query)
+                if i == 0 and side == 0:
+                    value_sum[...] = value_part
+                    key_sum[...] = key_part
+                else:
+                    value_sum[...] += value_part
+                    key_sum[...] += key_part
+                query_t[mine, at] = dot(keys_t[mine], grad_scores)
+        turned = key_sum[...]
+        turned = turned * cosine[...] - partner(turned) * sine[...]
+        out[:, group + j * LANES : group + (j + 1) * LANES] = turned.astype(bf16)
+        out[:, 2 * group + j * LANES : 2 * group + (j + 1) * LANES] = value_sum[...].astype(bf16)
+        turned = jnp.transpose(query_t[cols, :]) * (1.0 / math.sqrt(HEAD_DIM))
+        turned = turned * cosine[...] - partner(turned) * sine[...]
+        out[:, cols] = turned.astype(bf16)
+
+
+def middle_kernel(
+    me, source, p0, p1, p2, p3, out_all, scale, shift, mixed, middle, input_b, keep, give
+):
+    core, place = me[1], me[2]
+    group = p0.shape[1]
+    for s, piece in enumerate((p0, p1, p2, p3)):
+        mixed[:, lanes(lax.rem(place - s + 4, 4) * group, group)] = piece[...]
+    value = source[...].astype(f32) + dot(mixed[...], out_all[...])
+    middle[...] = value
+    normed, _ = normalize(value)
+    input_b[...] = (normed * (1.0 + scale[...]) + shift[...]).astype(bf16)
+    part = out_all.shape[0] // 8
+    for chip in range(4):
+        at = slice(chip * part, (chip + 1) * part)
+        keep[:, at] = mixed[:, lanes((2 * chip + core) * part, part)]
+        give[:, at] = mixed[:, lanes((2 * chip + 1 - core) * part, part)]
+
+
+def ffn_kernel(
+    me, in_own, in_other, cot_own, cot_other, own, on_x, on_y, top, low,
+    out_own, out_give, grad_own, grad_give, hidden, grad_upper, out_sum, grad_sum,
+):
+    chip = me[0]
+    rows, width = in_own.shape
+    units = low.shape[0]
+    depth = top.shape[0] // 2
+    inputs = jnp.concatenate([in_own[...], in_other[...]], axis=0)
+    cot = jnp.concatenate([cot_own[...], cot_other[...]], axis=0)
+    for r, block in enumerate((own, on_x, on_y, low)):
+        owner = chip ^ r
+        at = (pl.ds(pl.multiple_of((owner // 2) * depth, depth), depth), lanes((owner % 2) * units, units))
+        upper = None
+        for r2, up in enumerate((own, on_x, on_y, top)):
+            left = jnp.concatenate(
+                [ref[:, lanes((chip ^ r2) * depth, depth)] for ref in (in_own, in_other)], axis=0
+            )
+            term = dot(left, up[at])
+            upper = term if upper is None else upper + term
+        bell = 0.5 + 0.5 * lax.erf(upper * math.sqrt(0.5))
+        value = (upper * bell).astype(bf16)
+        slope = bell + upper * jnp.exp(upper * upper * -0.5) * (1.0 / math.sqrt(2.0 * math.pi))
+        down = block[...] if r == 3 else block[2 * depth :, :]
+        grad = (dot(cot, down, NT) * slope).astype(bf16)
+        hidden[:, r * units : (r + 1) * units] = value
+        grad_upper[:, lanes(owner * units, units)] = grad
+        term = dot(value, down)
+        if r:
+            out_sum[...] += term
+        else:
+            out_sum[...] = term
+        for r2, up in enumerate((own, on_x, on_y, top)):
+            cols = lanes((chip ^ r2) * depth, depth)
+            term = dot(grad, up[at], NT)
+            if r:
+                grad_sum[:, cols] += term
+            else:
+                grad_sum[:, cols] = term
+    out_own[...] = out_sum[:rows, :]
+    out_give[...] = out_sum[rows:, :].astype(bf16)
+    grad_own[...] = grad_sum[:rows, :]
+    grad_give[...] = grad_sum[rows:, :].astype(bf16)
+
+
+def grad_down_kernel(me, hidden, cot_own, cot_other, send_x, send_y, late_x, late_y, own):
+    rows = cot_own.shape[0]
+    units = own.shape[0]
+    half = units // 2
+
+    def block(r):
+        cols = slice(r * units, (r + 1) * units)
+        return dot(hidden[:rows, cols], cot_own[...], TN) + dot(
+            hidden[rows:, cols], cot_other[...], TN
+        )
+
+    across = block(3).astype(bf16)
+    send_x[:half, :] = across[:half]
+    send_y[:half, :] = across[half:]
+    on_x = block(1).astype(bf16)
+    send_x[half:, :] = on_x[:half]
+    late_x[...] = on_x[half:]
+    on_y = block(2).astype(bf16)
+    send_y[half:, :] = on_y[half:]
+    late_y[...] = on_y[:half]
+    own[...] = block(0)
+
+
+def grad_up_kernel(
+    me, in_own, in_other, grad_upper, mixed_own, mixed_other, branch_own, branch_other,
+    send_x, send_y, late_x, late_y, own,
+):
+    chip = me[0]
+    rows, width = in_own.shape
+    depth = width // 4
+    part = mixed_own.shape[1] // 4
+    half = part // 2
+
+    def block(r):
+        cols = lanes((chip ^ r) * depth, depth)
+        up = dot(in_own[:, cols], grad_upper[:rows, :], TN) + dot(
+            in_other[:, cols], grad_upper[rows:, :], TN
+        )
+        cols = lanes((chip ^ r) * part, part)
+        proj = dot(mixed_own[:, cols], branch_own[...], TN) + dot(
+            mixed_other[:, cols], branch_other[...], TN
+        )
+        return (up[:, :width], proj[:half]), (up[:, width:], proj[half:])
+
+    def put(ref, slot, count, pair):
+        ref[slot * depth : (slot + 1) * depth, :] = pair[0].astype(ref.dtype)
+        at = count * depth + slot * half
+        ref[at : at + half, :] = pair[1].astype(ref.dtype)
+
+    top, low = block(3)
+    put(send_x, 0, 2, top)
+    put(send_y, 0, 2, low)
+    top, low = block(1)
+    put(send_x, 1, 2, top)
+    put(late_x, 0, 1, low)
+    top, low = block(2)
+    put(late_y, 0, 1, top)
+    put(send_y, 1, 2, low)
+    top, low = block(0)
+    put(own, 0, 2, top)
+    put(own, 1, 2, low)
+
+
+def back_b_kernel(
+    me, grad_own, grad_take, out_own, out_take, middle, cot, scale, out_all,
+    result, grad_middle, branch, sums, g0, g1, g2, g3,
+):
+    place = me[2]
+    group = g0.shape[1]
+    result[...] = (middle[...] + out_own[...] + out_take[...].astype(f32)).astype(bf16)
+    normed, inverse = normalize(middle[...])
+    grad_in = grad_own[...] + grad_take[...].astype(f32)
+    sums[0:1, :] = jnp.sum(grad_in * normed, axis=0, keepdims=True)
+    sums[1:2, :] = jnp.sum(grad_in, axis=0, keepdims=True)
+    grad = cot[...].astype(f32) + norm_back(grad_in * (1.0 + scale[...]), normed, inverse)
+    grad_middle[...] = grad
+    low = grad.astype(bf16)
+    branch[...] = low
+    for s, piece in enumerate((g0, g1, g2, g3)):
+        at = pl.ds(pl.multiple_of(lax.rem(place - s + 4, 4) * group, group), group)
+        piece[...] = dot(low, out_all[at, :], NT).astype(bf16)
+
+
+def back_a_kernel(me, grad_projected, weight, normed, own, right, left, across, sums):
+    rows = own.shape[0]
+    first = second = None
+    for s, out in ((3, right), (1, left), (2, across), (0, own)):
+        at = slice(s * rows, (s + 1) * rows)
+        grad = dot(grad_projected[at, :], weight[...], NT)
+        out[...] = grad.astype(out.dtype)
+        one = jnp.sum(grad * normed[at, :], axis=0, keepdims=True)
+        two = jnp.sum(grad, axis=0, keepdims=True)
+        first, second = (one, two) if first is None else (first + one, second + two)
+    sums[0:1, :] = first
+    sums[1:2, :] = second
+
+
+def grad_qkv_kernel(me, input_a, grad_projected, keep, give):
+    core = me[1]
+    part = keep.shape[0] // 4
+    for out, owner in ((give, 1 - core), (keep, core)):
+        for chip in range(4):
+            cols = lanes((2 * chip + owner) * part, part)
+            out[chip * part : (chip + 1) * part, :] = dot(
+                input_a[:, cols], grad_projected[...], TN
+            ).astype(out.dtype)
+
+
+def pair_kernel(me, keep, take, send_x, send_y, late_x, late_y, own):
+    chip = me[0]
+    part = own.shape[0]
+    half = part // 2
+
+    def block(r, low):
+        at = pl.ds(pl.multiple_of((chip ^ r) * part + low * half, half), half)
+        return keep[at, :] + take[at, :].astype(f32)
+
+    send_x[:half, :] = block(3, 0).astype(bf16)
+    send_x[half:, :] = block(1, 0).astype(bf16)
+    send_y[:half, :] = block(3, 1).astype(bf16)
+    send_y[half:, :] = block(2, 1).astype(bf16)
+    late_x[...] = block(1, 1).astype(bf16)
+    late_y[...] = block(2, 0).astype(bf16)
+    own[:half, :] = block(0, 0)
+    own[half:, :] = block(0, 1)
+
+
+def tokens_kernel(me, own, right, left, source, scale, grad_middle, out):
+    grad_in = own[...] + right[...].astype(f32) + left[...].astype(f32)
+    normed, inverse = normalize(source[...].astype(f32))
+    out[...] = grad_middle[...] + norm_back(grad_in * (1.0 + scale[...]), normed, inverse)
+
+
+def finish_qkv_kernel(me, p0, p1, p2, p3, out):
+    place = me[2]
+    group = p0.shape[1] // 3
+    width = out.shape[1] // 3
+    for s, piece in enumerate((p0, p1, p2, p3)):
+        for part in range(3):
+            at = part * width + lax.rem(place - s + 4, 4) * group
+            out[:, lanes(at, group)] = piece[:, part * group : (part + 1) * group].astype(f32)
+
+
+def finish_up_kernel(me, inner0, inner1, outer0, outer1, up, proj):
+    core, place = me[1], me[2]
+    rows = up.shape[0]
+    units = up.shape[1] // 8
+    ends = (place == 0) | (place == 3)
+    total = [
+        jnp.where(ends, outer[...].astype(f32), inner[...])
+        for inner, outer in ((inner0, outer0), (inner1, outer1))
+    ]
+    for half in range(2):
+        for side, owner in ((0, core), (1, 1 - core)):
+            for n in range(2):
+                up[:, lanes((2 * (2 * half + n) + owner) * units, units)] = total[half][
+                    side * rows : (side + 1) * rows, n * units : (n + 1) * units
+                ]
+        proj[half * (rows // 2) : (half + 1) * (rows // 2), :] = total[half][2 * rows :, :]
+
+
+def after(values_in, *others):
+    return lax.optimization_barrier((values_in,) + others)[0]
+
+
+def relay_sums(send_x, send_y, late_x, late_y, own, splits):
+    got_x, got_y = hop(send_x, 2), hop(send_y, 4)
+    far_x, far_y, near_x, near_y, at = [], [], [], [], 0
+    for size in splits:
+        far_x.append(got_x[at : at + size])
+        far_y.append(got_y[at : at + size])
+        near_x.append(got_x[at + size : at + 2 * size])
+        near_y.append(got_y[at + size : at + 2 * size])
+        at += 2 * size
+    join = partial(jnp.concatenate, axis=0)
+    next_x = (late_x.astype(f32) + join(far_y).astype(f32)).astype(bf16)
+    next_y = (late_y.astype(f32) + join(far_x).astype(f32)).astype(bf16)
+    last_x, last_y = hop(next_x, 2), hop(next_y, 4)
+    out, at, seen = [], 0, 0
+    for n, size in enumerate(splits):
+        top = own[at : at + size] + near_x[n].astype(f32) + last_y[seen : seen + size].astype(f32)
+        low = (
+            own[at + size : at + 2 * size]
+            + near_y[n].astype(f32)
+            + last_x[seen : seen + size].astype(f32)
+        )
+        out.append((top, low))
+        at += 2 * size
+        seen += size
+    return out, (got_x, got_y)
+
+
+def line_sum(values_in):
+    inner = lax.ppermute(values_in.astype(bf16), "seq", [(0, 1), (3, 2)])
+    pair = values_in + inner.astype(f32)
+    across = lax.ppermute(pair.astype(bf16), "seq", [(1, 2), (2, 1)])
+    total = pair + across.astype(f32)
+    return total, lax.ppermute(total.astype(bf16), "seq", [(1, 0), (2, 3)])
+
+
+def per_device(tokens, noise_steps, w_qkv, w_out, w_up, w_down, w_time, cotangent):
+    index, place = lax.axis_index("dp"), lax.axis_index("seq")
+    me = jnp.stack([index // 2, index % 2, place]).astype(jnp.int32)
+    core = index % 2
+    _, rows, width = tokens.shape
+    group = width // 4
+    count = 4 * rows
+    hidden_units = w_up.shape[1]
+    part = w_out.shape[0]
+    source, cot = tokens[0], cotangent[0]
+
+    upper1, lower1 = shift(source, -1), shift(source, 1)
+    first, up_keep, up_give = call(
+        pack_kernel,
+        "pack",
+        [((part, 3 * group + width), bf16)] + [((part, hidden_units // 2), bf16)] * 2,
+        me,
+        w_qkv,
+        w_out,
+        w_up,
+    )
+    first_x, first_y = hop(first, 2), hop(first, 4)
+    up_take = hop(up_give, 1)
+    cot_other = hop(cot, 1)
+    (ffn,) = call(
+        pack_ffn_kernel,
+        "pack_ffn",
+        [((4 * part + w_down.shape[0], hidden_units // 4), bf16)],
+        me,
+        up_keep,
+        up_take,
+        w_down,
+    )
+    steps_all = lax.all_to_all(
+        jnp.broadcast_to(noise_steps.astype(f32), (8,)),
+        "dp",
+        split_axis=0,
+        concat_axis=0,
+        tiled=True,
+    )
+    embed_all = time_embedding(steps_all)
+    cond_part = jnp.dot(embed_all, w_time.astype(f32), precision=highest)
+    condition = lax.all_to_all(cond_part, "dp", split_axis=0, concat_axis=0, tiled=True).reshape(
+        4, width
+    )
+    scale_a, shift_a, scale_b, shift_b = [condition[i : i + 1] for i in range(4)]
+    upper1, lower1, first_x, first_y = lax.optimization_barrier(
+        (upper1, lower1, first_x, first_y)
+    )
+    upper2, lower2 = shift(upper1, -1), shift(lower1, 1)
+    first_top, first_low = hop(first_y[: part // 2], 2), hop(first_x[part // 2 :], 4)
+    ffn = after(ffn, first_x)
+    ffn_x, ffn_y = hop(ffn, 2), hop(ffn, 4)
+    upper2, lower2, first_top, first_low = lax.optimization_barrier(
+        (upper2, lower2, first_top, first_low)
+    )
+    upper3, lower3 = shift(upper2, -1), shift(lower2, 1)
+    mine = (first, first_x, first_y, first_top, first_low)
+    theirs = [hop(piece, 1) for piece in mine]
+    qkv_all, out_all = call(
+        unpack_kernel,
+        "unpack",
+        [((width, 3 * group), bf16), ((width, width), bf16)],
+        me,
+        *mine,
+        *theirs,
+    )
+    half = HEAD_DIM // 2
+    frequency = jnp.exp(-math.log(10000.0) * jnp.arange(half, dtype=f32) / half)
+    block_place = (place + jnp.arange(4)) % 4
+    positions = (block_place[:, None] * rows + jnp.arange(rows)).reshape(-1).astype(f32)
+    angles = positions[:, None] * frequency
+    cosine, sine = jnp.cos(angles), jnp.sin(angles)
+    cosine = jnp.concatenate([cosine] * 4, axis=1)
+    sine = jnp.concatenate([-sine, sine] * 2, axis=1)
+
+    normed_a, input_a, queries, keys, values = call(
+        qkv_kernel,
+        "qkv",
+        [((count, width), f32), ((count, width), bf16)] + [((count, group), bf16)] * 3,
+        me,
+        source,
+        upper1,
+        upper2,
+        upper3,
+        lower1,
+        lower2,
+        lower3,
+        scale_a,
+        shift_a,
+        qkv_all,
+        cosine,
+        sine,
+        flops=6 * count * width * group,
+    )
+    attended, log_total = call(
+        attend_kernel,
+        "attend",
+        [((count, group), bf16), ((8, count), f32)],
+        me,
+        queries,
+        keys,
+        values,
+        flops=16 * count * count * group,
+    )
+    attended, ffn_x, ffn_y = lax.optimization_barrier((attended, ffn_x, ffn_y))
+    cut = ffn.shape[0] // 2
+    ffn_top, ffn_low = hop(ffn_y[:cut], 2), hop(ffn_x[cut:], 4)
+    pieces = [attended[:rows]] + [
+        turn(attended[s * rows : (s + 1) * rows], s) for s in range(1, 4)
+    ]
+    mixed, middle, input_b, mixed_keep, mixed_give = call(
+        middle_kernel,
+        "middle",
+        [((rows, width), bf16), ((rows, width), f32), ((rows, width), bf16)]
+        + [((rows, width // 2), bf16)] * 2,
+        me,
+        source,
+        *pieces,
+        out_all,
+        scale_b,
+        shift_b,
+        flops=2 * rows * width * width,
+    )
+    input_other = hop(input_b, 1)
+    mixed_take = hop(mixed_give, 1)
+
+    units = hidden_units // 2
+    out_own, out_give, grad_own, grad_give, hidden, grad_upper = call(
+        ffn_kernel,
+        "ffn",
+        [((rows, width), f32), ((rows, width), bf16)] * 2 + [((2 * rows, units), bf16)] * 2,
+        me,
+        input_b,
+        input_other,
+        cot,
+        cot_other,
+        ffn,
+        ffn_x,
+        ffn_y,
+        ffn_top,
+        ffn_low,
+        scratch=[pltpu.VMEM((2 * rows, width), f32)] * 2,
+        flops=16 * rows * width * units,
+    )
+    grad_take, out_take = hop(grad_give, 1), hop(out_give, 1)
+    down_rows = w_down.shape[0]
+    down_parts = call(
+        grad_down_kernel,
+        "grad_down",
+        [((down_rows, width), bf16)] * 2
+        + [((down_rows // 2, width), bf16)] * 2
+        + [((down_rows, width), f32)],
+        me,
+        hidden,
+        cot,
+        cot_other,
+        flops=4 * rows * width * units,
+    )
+    down_sums, down_first = relay_sums(*down_parts, (down_rows // 2,))
+    result, grad_middle, branch, sums_b, *to_heads = call(
+        back_b_kernel,
+        "back_b",
+        [((rows, width), bf16), ((rows, width), f32), ((rows, width), bf16), ((2, width), f32)]
+        + [((rows, group), bf16)] * 4,
+        me,
+        grad_own,
+        grad_take,
+        out_own,
+        out_take,
+        middle,
+        cot,
+        scale_b,
+        out_all,
+        flops=2 * rows * width * width,
+    )
+    grad_heads = [to_heads[0]] + [turn(to_heads[s], -s) for s in range(1, 4)]
+    branch_other = hop(branch, 1)
+    up_rows = 2 * width // 4 + part
+    up_parts = call(
+        grad_up_kernel,
+        "grad_up",
+        [((up_rows, width), bf16)] * 2
+        + [((up_rows // 2, width), bf16)] * 2
+        + [((up_rows, width), f32)],
+        me,
+        input_b,
+        input_other,
+        grad_upper,
+        mixed_keep,
+        mixed_take,
+        branch,
+        branch_other,
+        flops=4 * rows * width * units,
+    )
+    up_x, up_y = after(up_parts[0], down_first[0]), after(up_parts[1], down_first[1])
+    up_sums, _ = relay_sums(up_x, up_y, *up_parts[2:], (width // 4, part // 2))
+    (grad_projected,) = call(
+        attend_back_kernel,
+        "attend_back",
+        [((count, 3 * group), bf16)],
+        me,
+        queries,
+        keys,
+        values,
+        *grad_heads,
+        log_total,
+        cosine,
+        sine,
+        scratch=[pltpu.VMEM((count, LANES), f32)] * 2 + [pltpu.VMEM((group, count), f32)],
+        flops=40 * count * count * group,
+    )
+    grad_a, right, left, across, sums_a = call(
+        back_a_kernel,
+        "back_a",
+        [((rows, width), f32)] + [((rows, width), bf16)] * 2 + [((rows, width), bf16), ((2, width), f32)],
+        me,
+        grad_projected,
+        qkv_all,
+        normed_a,
+        flops=6 * count * width * group,
+    )
+    got_right, got_left = shift(right, 1), shift(left, -1)
+    keep, give = call(
+        grad_qkv_kernel,
+        "grad_qkv",
+        [((width // 2, 3 * group), f32), ((width // 2, 3 * group), bf16)],
+        me,
+        input_a,
+        grad_projected,
+        flops=6 * count * width * group,
+    )
+    qkv_parts = call(
+        pair_kernel,
+        "pair",
+        [((part, 3 * group), bf16)] * 2
+        + [((part // 2, 3 * group), bf16)] * 2
+        + [((part, 3 * group), f32)],
+        me,
+        keep,
+        hop(give, 1),
+    )
+    qkv_sums, _ = relay_sums(*qkv_parts, (part // 2,))
+    got_right, got_left = (
+        shift((across.astype(f32) + got_right.astype(f32)).astype(bf16), 1),
+        shift((across.astype(f32) + got_left.astype(f32)).astype(bf16), -1),
+    )
+    got_right, got_left = (
+        shift((left.astype(f32) + got_right.astype(f32)).astype(bf16), 1),
+        shift((right.astype(f32) + got_left.astype(f32)).astype(bf16), -1),
+    )
+    (grad_tokens,) = call(
+        tokens_kernel,
+        "tokens",
+        [((rows, width), f32)],
+        me,
+        grad_a,
+        got_right,
+        got_left,
+        source,
+        scale_a,
+        grad_middle,
+    )
+
+    ends = (place == 0) | (place == 3)
+    down_lines = [line_sum(piece) for piece in down_sums[0]]
+    grad_down = jnp.concatenate(
+        [jnp.where(ends, outer.astype(f32), inner) for inner, outer in down_lines], axis=0
+    )
+    up_lines = []
+    for n in range(2):
+        rows_both = up_sums[0][n].reshape(2, part, width)
+        own_rows = lax.dynamic_index_in_dim(rows_both, core, 0, keepdims=False)
+        other_rows = lax.dynamic_index_in_dim(rows_both, 1 - core, 0, keepdims=False)
+        taken = hop(other_rows.astype(bf16), 1).astype(f32)
+        up_lines.append(line_sum(jnp.concatenate([own_rows, taken, up_sums[1][n]], axis=0)))
+    grad_up, grad_proj = call(
+        finish_up_kernel,
+        "finish_up",
+        [((part, hidden_units), f32), ((part, width), f32)],
+        me,
+        up_lines[0][0],
+        up_lines[1][0],
+        up_lines[0][1],
+        up_lines[1][1],
+    )
+    qkv_cols = jnp.concatenate(qkv_sums[0], axis=0).astype(bf16)
+    (grad_qkv,) = call(
+        finish_qkv_kernel,
+        "finish_qkv",
+        [((part, 3 * width), f32)],
+        me,
+        qkv_cols,
+        *[turn(qkv_cols, s) for s in range(1, 4)],
+    )
+    grad_condition = jnp.concatenate([sums_a, sums_b], axis=0)
+    cond_cols = lax.all_to_all(
+        grad_condition.reshape(8, -1), "dp", split_axis=0, concat_axis=0, tiled=True
+    )
+    cond_sum = cond_cols
+    for s in range(1, 4):
+        cond_sum = cond_sum + turn(cond_cols, s)
+    grad_time = jnp.dot(embed_all.T, cond_sum, precision=highest)
+    return (result[None], grad_tokens[None], grad_qkv, grad_proj, grad_up, grad_down, grad_time)
+
+
 def solution(mesh):
     in_specs = (
         P("dp", "seq", None),
@@ -406,6 +1162,7 @@
         P("dp", None),
         P(None, "dp"),
     )
+    square = mesh.shape["dp"] == 8 and mesh.shape["seq"] == 4
     return jax.shard_map(
-        per_device, mesh=mesh, in_specs=in_specs, out_specs=out_specs, check_vma=False
-    )
+        per_device if square else per_device_any, mesh=mesh, in_specs=in_specs, out_specs=out_specs, check_vma=False
+    )

time: 609 us -> 459 us (0.75)
  matrix products: 84.3 us -> 1.62 us
  other arithmetic: 98.1 us -> 18.2 us
  Pallas kernels: 0 us -> 71 us
  local copies, waits for them, and re-layouts: 90.9 us -> 42.1 us
  starting transfers between devices: 119 us -> 108 us
    dot_general x18 -> x0, matrix products: 82.7 us -> none  [the longest x1 13.1 us: attend_backward(): jnp.einsum('qhd,khd->hqk', grad_attn, values, preferred_element_type=f32)]
    pallas_call x0 -> x17, Pallas kernels: none -> 71 us  [call(): pl.pallas_call(kernel, name=name, out_shape=[jax.ShapeDtypeStruct(shape,...]
    ppermute x18 -> x12, waiting for transfers between devices: 75.2 us -> 9.69 us  [shift(): lax.ppermute(values_in, 'seq', [(i, i + step) for i in range(count) if 0...]
    ppermute x42 -> x35, waiting for transfers between devices: 61.8 us -> 110 us  [hop(): return lax.ppermute(values_in, 'dp', [(i, i ^ bit) for i in range(count)])]
    convert_element_type x18 -> x22, other arithmetic: 37.1 us -> 7.78 us  [the longest x3 2.01 us: line_sum(): inner = lax.ppermute(values_in.astype(bf16), 'seq', [(0, 1), (3, 2)])]
    unnamed x200 -> x162, local copies, waits for them, and re-layouts: 13.9 us -> 36.6 us
    ppermute x9 -> x12, waiting for transfers between devices: 1.65 us -> 21.7 us  [turn(): lax.ppermute(values_in, 'seq', [(i, (i + step) % count) for i in range(co...]
    dynamic_update_slice x19 -> x0, local copies, waits for them, and re-layouts: 19.8 us -> none  [gather_chips(): lax.dynamic_update_slice_in_dim(out, piece, (chip ^ other) * rows + shift...]
  transfers between devices with their start and end apart: 81 -> 74, of which waited for: 25 -> 29; matrix products, arithmetic and copies ran while one was open for 42% -> 5% of each run, Pallas kernels for 0% -> 12%
where the time goes in v2:
time: 459 us; the launch traced here: 454 us
  waiting for transfers between devices  210 us (46%)
  starting transfers between devices  108 us (24%)
  Pallas kernels  71 us (15%)
  local copies, waits for them, and re-layouts  42.1 us (9%)
  other arithmetic  18.2 us (4%)
    ppermute x35, waiting for transfers between devices, hop(): return lax.ppermute(values_in, 'dp', [(i, i ^ bit) for i in range(count)])  110 us
    pallas_call x17, Pallas kernels, call(): pl.pallas_call(kernel, name=name, out_shape=[jax.ShapeDtypeStruct(shape,...  71 us
    ppermute x4, waiting for transfers between devices, line_sum(): return (total, lax.ppermute(total.astype(bf16), 'seq', [(1, 0), (2, 3)]))  45.1 us
    unnamed x162, local copies, waits for them, and re-layouts  36.6 us
    ppermute x12, starting transfers between devices, shift(): lax.ppermute(values_in, 'seq', [(i, i + step) for i in range(count) if 0...  31.7 us
    ppermute x35, starting transfers between devices, hop(): return lax.ppermute(values_in, 'dp', [(i, i ^ bit) for i in range(count)])  27.8 us
    ppermute x4, waiting for transfers between devices, line_sum(): inner = lax.ppermute(values_in.astype(bf16), 'seq', [(0, 1), (3, 2)])  23.5 us
    ppermute x12, waiting for transfers between devices, turn(): lax.ppermute(values_in, 'seq', [(i, (i + step) % count) for i in range(co...  21.7 us
  transfers between devices with their start and end apart: 74, of which 29 were waited for; matrix products, arithmetic and copies ran while one was open for 5% of the time, Pallas kernels for 12%

profile of v2, /device:TPU:0, one launch (start us, length us, event | category | flops | bytes accessed | tf_op | source)
XLA Modules:
  0.0 454.1 jit_solution(14526869480127173785)
XLA Ops:
  2.1 5.6 %collective-permute-start.1 = (bf16[256,1024]{1,0:T(8,128)(2,1)}, bf16[256,1024]{1,0:T(8,128)(2,1)S(1)}, u32[]{:S(2)}, u32[]{:S(2)}) collective-permute-start(bf16[256,1024]{1,0:T(8,128)(2,1)} %bitcast.35), channel_id=1, source_target_pairs={{0,1},{1,2},{2,3},{4,5},{5,6},{6,7},{8,9},{9,10},{10,11},{12,13},{... | collective-permute-start | bytes 1572872 | tf_op jit(solution)/shard_map/ppermute | solution.py:137
  16.9 8.7 %collective-permute-done.2.refs_1_ = bf16[128,1792]{1,0:T(8,128)(2,1)S(1)} collective-permute-done((bf16[128,1792]{1,0:T(8,128)(2,1)}, bf16[128,1792]{1,0:T(8,128)(2,1)S(1)}, u32[]{:S(2)}, u32[]{:S(2)}) %collective-permute-start.2) | collective-permute-done | bytes 458784 | tf_op jit(solution)/shard_map/ppermute | solution.py:59
  29.6 5.4 %collective-permute-start.5 = (bf16[256,1024]{1,0:T(8,128)(2,1)S(1)}, bf16[256,1024]{1,0:T(8,128)(2,1)}, u32[]{:S(2)}, u32[]{:S(2)}) collective-permute-start(bf16[256,1024]{1,0:T(8,128)(2,1)S(1)} %collective-permute-done.1.refs_4_), channel_id=1, source_target_pairs={{0,1},{1,2},{2,3},{4,5},{5,6},{6,7},{8,9},{9,10},{10,11},{12,13},{... | collective-permute-start | bytes 1572872 | tf_op jit(solution)/shard_map/ppermute | solution.py:137
  36.2 3.8 all-to-all-start
  47.7 50.5 %collective-permute-done.7.refs_4_ = bf16[64,1792]{1,0:T(8,128)(2,1)} collective-permute-done((bf16[64,1792]{1,0:T(8,128)(2,1)S(1)}, bf16[64,1792]{1,0:T(8,128)(2,1)}, u32[]{:S(2)}, u32[]{:S(2)}) %collective-permute-start.7) | collective-permute-done | bytes 229408 | tf_op jit(solution)/shard_map/ppermute | solution.py:59
  104.8 5.4 %collective-permute-start.9 = (bf16[256,1024]{1,0:T(8,128)(2,1)}, bf16[256,1024]{1,0:T(8,128)(2,1)}, u32[]{:S(2)}, u32[]{:S(2)}) collective-permute-start(bf16[256,1024]{1,0:T(8,128)(2,1)} %collective-permute-done.5.refs_5_), channel_id=1, source_target_pairs={{0,1},{1,2},{2,3},{4,5},{5,6},{6,7},{8,9},{9,10},{10,11},{12,13},{... | collective-permute-start | bytes 1572872 | tf_op jit(solution)/shard_map/ppermute | solution.py:137
  111.1 3.8 all-to-all-start.1
  116.1 4.0 pad_maximum_fusion.3
  129.4 5.1 %qkv.1 = (f32[1024,1024]{1,0:T(8,128)S(1)}, bf16[1024,1024]{1,0:T(8,128)(2,1)S(1)}, bf16[1024,256]{1,0:T(8,128)(2,1)S(1)}, bf16[1024,256]{1,0:T(8,128)(2,1)S(1)}, bf16[1024,256]{1,0:T(8,128)(2,1)S(1)}) custom-call(s32[3]{0:T(128)S(1)} %pad_add_fusion.me, bf16[256,1024]{1,0:T(8,128)(2,1)S(1)} %bitcast.36, bf16[256,1024]{1,0:T(8,128)(2,1)S(1)} %copy-done.36, ...), custom_call_target="tpu_custom_call" | custom-call | flops 1610612736 | bytes 6299648 | tf_op jit(solution)/shard_map/qkv/pallas_call | solution.py:400
  134.5 6.7 %attend.1 = (bf16[1024,256]{1,0:T(8,128)(2,1)S(1)}, f32[8,1024]{1,0:T(8,128)S(1)}) custom-call(s32[3]{0:T(128)S(1)} %pad_add_fusion.me, bf16[1024,256]{1,0:T(8,128)(2,1)S(1)} %get-tuple-element.85.queries, bf16[1024,256]{1,0:T(8,128)(2,1)S(1)} %get-tuple-element.86.keys, bf16[1024,256]{1,0:T(8,128)(2,1)S(1)} %get-tuple-element.87.values), custom_call_target="tpu_custom_call" | custom-call | flops 4294967296 | bytes 1572864 | tf_op jit(solution)/shard_map/attend/pallas_call | solution.py:400
  155.6 4.5 collective-permute-done.19.p2
  170.8 14.1 %ffn.1 = (f32[256,1024]{1,0:T(8,128)S(1)}, bf16[256,1024]{1,0:T(8,128)(2,1)}, f32[256,1024]{1,0:T(8,128)S(1)}, bf16[256,1024]{1,0:T(8,128)(2,1)}, bf16[512,2048]...) custom-call(s32[3]{0:T(128)S(1)} %pad_add_fusion.me, bf16[256,1024]{1,0:T(8,128)(2,1)S(1)} %get-tuple-element.94.in_own, ...), custom_call_target="tpu_custom_call" | custom-call | flops 8589934592 | bytes 10485760 | tf_op jit(solution)/shard_map/ffn/pallas_call | solution.py:400
  197.3 3.9 back_b.1
  206.0 3.8 grad_down.1
  211.9 4.1 collective-permute-done.28.g2
  216.1 13.1 %attend_back.1.grad_projected = bf16[1024,768]{1,0:T(8,128)(2,1)S(1)} custom-call(s32[3]{0:T(128)S(1)} %pad_add_fusion.me, bf16[1024,256]{1,0:T(8,128)(2,1)S(1)} %copy-done.63, bf16[1024,256]{1,0:T(8,128)(2,1)S(1)} %copy-done.65, bf16[1024,256]{1,0:T(8,128)(2,1)S(1)} %copy-done.67, bf16[256,256]{1,0:T(8,128)(2,1)S(1)} %get-tuple-element.103.g0, ...), custom_call_target="tpu_custom_call" | custom-call | flops 10737418240 | bytes 3178496 | tf_op jit(solution)/shard_map/attend_back/pallas_call | solution.py:400
  235.1 3.3 all-to-all-start.2
  252.9 4.3 grad_up.1
  261.6 3.2 collective-permute-done.68
  277.4 6.9 %collective-permute-done.60 = bf16[256,1024]{1,0:T(8,128)(2,1)S(1)} collective-permute-done((bf16[256,1024]{1,0:T(8,128)(2,1)S(1)}, bf16[256,1024]{1,0:T(8,128)(2,1)S(1)}, u32[]{:S(2)}, u32[]{:S(2)}) %collective-permute-start.60) | collective-permute-done | bytes 524320 | tf_op jit(solution)/shard_map/ppermute | solution.py:59
  289.5 24.3 %collective-permute-done.39 = bf16[128,768]{1,0:T(8,128)(2,1)S(1)} collective-permute-done((bf16[128,768]{1,0:T(8,128)(2,1)S(1)}, bf16[128,768]{1,0:T(8,128)(2,1)S(1)}, u32[]{:S(2)}, u32[]{:S(2)}) %collective-permute-start.39) | collective-permute-done | bytes 196640 | tf_op jit(solution)/shard_map/ppermute | solution.py:59
  315.5 5.0 %collective-permute-done.37 = bf16[128,768]{1,0:T(8,128)(2,1)S(1)} collective-permute-done((bf16[128,768]{1,0:T(8,128)(2,1)S(1)}, bf16[128,768]{1,0:T(8,128)(2,1)S(1)}, u32[]{:S(2)}, u32[]{:S(2)}) %collective-permute-start.37) | collective-permute-done | bytes 196640 | tf_op jit(solution)/shard_map/ppermute | solution.py:59
  332.4 5.5 %collective-permute-done.41.p1 = bf16[128,768]{1,0:T(8,128)(2,1)S(1)} collective-permute-done((bf16[128,768]{1,0:T(8,128)(2,1)S(1)}, bf16[128,768]{1,0:T(8,128)(2,1)S(1)}, u32[]{:S(2)}, u32[]{:S(2)}) %collective-permute-start.41) | collective-permute-done | bytes 196640 | tf_op jit(solution)/shard_map/ppermute | solution.py:132
  339.2 5.4 %collective-permute-start.65 = (bf16[256,1024]{1,0:T(8,128)(2,1)S(1)}, bf16[256,1024]{1,0:T(8,128)(2,1)S(1)}, u32[]{:S(2)}, u32[]{:S(2)}) collective-permute-start(bf16[256,1024]{1,0:T(8,128)(2,1)S(1)} %get-tuple-element.155), channel_id=1, source_target_pairs={{0,1},{3,2},{4,5},{7,6},{8,9},{11,10},{12,13},{15,14},{16,17},{19,... | collective-permute-start | bytes 1572872 | tf_op jit(solution)/shard_map/ppermute | solution.py:832
  349.8 4.6 %collective-permute-start.32 = (bf16[256,1024]{1,0:T(8,128)(2,1)S(1)}, bf16[256,1024]{1,0:T(8,128)(2,1)S(1)}, u32[]{:S(2)}, u32[]{:S(2)}) collective-permute-start(bf16[256,1024]{1,0:T(8,128)(2,1)S(1)} %add_convert_fusion.5), channel_id=1, source_target_pairs={{0,1},{1,2},{2,3},{4,5},{5,6},{6,7},{8,9},{9,10},{10,11},{12,13},{... | collective-permute-start | bytes 1572872 | tf_op jit(solution)/shard_map/ppermute | solution.py:137
  362.4 9.7 %collective-permute-done.32.right = bf16[256,1024]{1,0:T(8,128)(2,1)S(1)} collective-permute-done((bf16[256,1024]{1,0:T(8,128)(2,1)S(1)}, bf16[256,1024]{1,0:T(8,128)(2,1)S(1)}, u32[]{:S(2)}, u32[]{:S(2)}) %collective-permute-start.32) | collective-permute-done | bytes 524320 | tf_op jit(solution)/shard_map/ppermute | solution.py:137
  374.5 11.7 %collective-permute-done.56 = bf16[320,1024]{1,0:T(8,128)(2,1)S(1)} collective-permute-done((bf16[320,1024]{1,0:T(8,128)(2,1)S(1)}, bf16[320,1024]{1,0:T(8,128)(2,1)S(1)}, u32[]{:S(2)}, u32[]{:S(2)}) %collective-permute-start.56) | collective-permute-done | bytes 655392 | tf_op jit(solution)/shard_map/ppermute | solution.py:832
  387.0 10.0 %collective-permute-done.50 = bf16[320,1024]{1,0:T(8,128)(2,1)S(1)} collective-permute-done((bf16[320,1024]{1,0:T(8,128)(2,1)S(1)}, bf16[320,1024]{1,0:T(8,128)(2,1)S(1)}, u32[]{:S(2)}, u32[]{:S(2)}) %collective-permute-start.50) | collective-permute-done | bytes 655392 | tf_op jit(solution)/shard_map/ppermute | solution.py:832
  404.5 12.8 %collective-permute-done.63 = bf16[256,1024]{1,0:T(8,128)(2,1)S(1)} collective-permute-done((bf16[256,1024]{1,0:T(8,128)(2,1)S(1)}, bf16[256,1024]{1,0:T(8,128)(2,1)S(1)}, u32[]{:S(2)}, u32[]{:S(2)}) %collective-permute-start.63) | collective-permute-done | bytes 524320 | tf_op jit(solution)/shard_map/ppermute | solution.py:836
  417.7 10.9 %collective-permute-done.67 = bf16[256,1024]{1,0:T(8,128)(2,1)S(1)} collective-permute-done((bf16[256,1024]{1,0:T(8,128)(2,1)S(1)}, bf16[256,1024]{1,0:T(8,128)(2,1)S(1)}, u32[]{:S(2)}, u32[]{:S(2)}) %collective-permute-start.67) | collective-permute-done | bytes 524320 | tf_op jit(solution)/shard_map/ppermute | solution.py:836
  430.4 12.3 %collective-permute-done.59.outer1 = bf16[320,1024]{1,0:T(8,128)(2,1)S(1)} collective-permute-done((bf16[320,1024]{1,0:T(8,128)(2,1)S(1)}, bf16[320,1024]{1,0:T(8,128)(2,1)S(1)}, u32[]{:S(2)}, u32[]{:S(2)}) %collective-permute-start.59) | collective-permute-done | bytes 655392 | tf_op jit(solution)/shard_map/ppermute | solution.py:836
  442.6 9.1 %collective-permute-done.58.outer0 = bf16[320,1024]{1,0:T(8,128)(2,1)S(1)} collective-permute-done((bf16[320,1024]{1,0:T(8,128)(2,1)S(1)}, bf16[320,1024]{1,0:T(8,128)(2,1)S(1)}, u32[]{:S(2)}, u32[]{:S(2)}) %collective-permute-start.58) | collective-permute-done | bytes 655392 | tf_op jit(solution)/shard_map/ppermute | solution.py:836
  (353 shorter events, 169.9 us)
Async XLA Ops:
  0.6 26.4 %collective-permute-start = (bf16[256,1024]{1,0:T(8,128)(2,1)}, bf16[256,1024]{1,0:T(8,128)(2,1)S(1)}, u32[]{:S(2)}, u32[]{:S(2)}) collective-permute-start(bf16[256,1024]{1,0:T(8,128)(2,1)} %bitcast.34), channel_id=1, source_target_pairs={{1,0},{2,1},{3,2},{5,4},{6,5},{7,6},{9,8},{10,9},{11,10},{13,12},{... | collective-permute-start | bytes 1572872 | tf_op jit(solution)/shard_map/ppermute | solution.py:137
  2.1 25.0 %collective-permute-start.1 = (bf16[256,1024]{1,0:T(8,128)(2,1)}, bf16[256,1024]{1,0:T(8,128)(2,1)S(1)}, u32[]{:S(2)}, u32[]{:S(2)}) collective-permute-start(bf16[256,1024]{1,0:T(8,128)(2,1)} %bitcast.35), channel_id=1, source_target_pairs={{0,1},{1,2},{2,3},{4,5},{5,6},{6,7},{8,9},{9,10},{10,11},{12,13},{... | collective-permute-start | bytes 1572872 | tf_op jit(solution)/shard_map/ppermute | solution.py:137
  28.3 70.0 %collective-permute-start.4 = (bf16[256,1024]{1,0:T(8,128)(2,1)S(1)}, bf16[256,1024]{1,0:T(8,128)(2,1)}, u32[]{:S(2)}, u32[]{:S(2)}) collective-permute-start(bf16[256,1024]{1,0:T(8,128)(2,1)S(1)} %collective-permute-done.refs_1_), channel_id=1, source_target_pairs={{1,0},{2,1},{3,2},{5,4},{6,5},{7,6},{9,8},{10,9},{11,10},{13,12},{... | collective-permute-start | bytes 1572872 | tf_op jit(solution)/shard_map/ppermute | solution.py:137
  29.6 69.2 %collective-permute-start.5 = (bf16[256,1024]{1,0:T(8,128)(2,1)S(1)}, bf16[256,1024]{1,0:T(8,128)(2,1)}, u32[]{:S(2)}, u32[]{:S(2)}) collective-permute-start(bf16[256,1024]{1,0:T(8,128)(2,1)S(1)} %collective-permute-done.1.refs_4_), channel_id=1, source_target_pairs={{0,1},{1,2},{2,3},{4,5},{5,6},{6,7},{8,9},{9,10},{10,11},{12,13},{... | collective-permute-start | bytes 1572872 | tf_op jit(solution)/shard_map/ppermute | solution.py:137
  36.2 65.8 %all-to-all-start = ((f32[8,1,1]{2,1,0:T(1,128)}), f32[8,1,1]{2,1,0:T(1,128)S(1)}, u32[]{:S(2)}, u32[]{:S(2)}) async-start(f32[8,1,1]{2,1,0:T(1,128)} %broadcast_in_dim.9), calls=%async_computation | async-start | bytes 8192 | tf_op jit(solution)/shard_map/all_to_all | solution.py:872
  43.6 97.7 %collective-permute-start.16 = (bf16[1024,1024]{1,0:T(8,128)(2,1)}, bf16[1024,1024]{1,0:T(8,128)(2,1)}, u32[]{:S(2)}, u32[]{:S(2)}) collective-permute-start(bf16[1024,1024]{1,0:T(8,128)(2,1)} %pack_ffn.1.own), channel_id=1, source_target_pairs={{0,8},{4,12},{8,0},{12,4},{16,24},{20,28},{24,16},{28,20},{1,9},{5... | collective-permute-start | bytes 6291464 | tf_op jit(solution)/shard_map/ppermute | solution.py:59
  45.6 95.7 %collective-permute-start.17 = (bf16[1024,1024]{1,0:T(8,128)(2,1)}, bf16[1024,1024]{1,0:T(8,128)(2,1)}, u32[]{:S(2)}, u32[]{:S(2)}) collective-permute-start(bf16[1024,1024]{1,0:T(8,128)(2,1)} %pack_ffn.1.own), channel_id=1, source_target_pairs={{0,16},{4,20},{8,24},{12,28},{16,0},{20,4},{24,8},{28,12},{1,17},{... | collective-permute-start | bytes 6291464 | tf_op jit(solution)/shard_map/ppermute | solution.py:59
  47.1 51.2 %collective-permute-start.7 = (bf16[64,1792]{1,0:T(8,128)(2,1)S(1)}, bf16[64,1792]{1,0:T(8,128)(2,1)}, u32[]{:S(2)}, u32[]{:S(2)}) collective-permute-start(bf16[64,1792]{1,0:T(8,128)(2,1)S(1)} %slice.137), channel_id=1, source_target_pairs={{0,16},{4,20},{8,24},{12,28},{16,0},{20,4},{24,8},{28,12},{1,17},{... | collective-permute-start | bytes 688136 | tf_op jit(solution)/shard_map/ppermute | solution.py:59
  103.5 25.8 %collective-permute-start.8 = (bf16[256,1024]{1,0:T(8,128)(2,1)}, bf16[256,1024]{1,0:T(8,128)(2,1)}, u32[]{:S(2)}, u32[]{:S(2)}) collective-permute-start(bf16[256,1024]{1,0:T(8,128)(2,1)} %collective-permute-done.4.refs_2_), channel_id=1, source_target_pairs={{1,0},{2,1},{3,2},{5,4},{6,5},{7,6},{9,8},{10,9},{11,10},{13,12},{... | collective-permute-start | bytes 1572872 | tf_op jit(solution)/shard_map/ppermute | solution.py:137
  104.8 24.5 %collective-permute-start.9 = (bf16[256,1024]{1,0:T(8,128)(2,1)}, bf16[256,1024]{1,0:T(8,128)(2,1)}, u32[]{:S(2)}, u32[]{:S(2)}) collective-permute-start(bf16[256,1024]{1,0:T(8,128)(2,1)} %collective-permute-done.5.refs_5_), channel_id=1, source_target_pairs={{0,1},{1,2},{2,3},{4,5},{5,6},{6,7},{8,9},{9,10},{10,11},{12,13},{... | collective-permute-start | bytes 1572872 | tf_op jit(solution)/shard_map/ppermute | solution.py:137
  142.6 25.4 %collective-permute-start.23 = (bf16[512,1024]{1,0:T(8,128)(2,1)S(1)}, bf16[512,1024]{1,0:T(8,128)(2,1)S(1)}, u32[]{:S(2)}, u32[]{:S(2)}) collective-permute-start(bf16[512,1024]{1,0:T(8,128)(2,1)S(1)} %slice.150), channel_id=1, source_target_pairs={{0,8},{4,12},{8,0},{12,4},{16,24},{20,28},{24,16},{28,20},{1,9},{5... | collective-permute-start | bytes 3145736 | tf_op jit(solution)/shard_map/ppermute | solution.py:59
  145.7 25.2 %collective-permute-start.24 = (bf16[512,1024]{1,0:T(8,128)(2,1)S(1)}, bf16[512,1024]{1,0:T(8,128)(2,1)S(1)}, u32[]{:S(2)}, u32[]{:S(2)}) collective-permute-start(bf16[512,1024]{1,0:T(8,128)(2,1)S(1)} %slice.151), channel_id=1, source_target_pairs={{0,16},{4,20},{8,24},{12,28},{16,0},{20,4},{24,8},{28,12},{1,17},{... | collective-permute-start | bytes 3145736 | tf_op jit(solution)/shard_map/ppermute | solution.py:59
  190.1 55.4 %collective-permute-start.44 = (bf16[256,512]{1,0:T(8,128)(2,1)}, bf16[256,512]{1,0:T(8,128)(2,1)}, u32[]{:S(2)}, u32[]{:S(2)}) collective-permute-start(bf16[256,512]{1,0:T(8,128)(2,1)} %get-tuple-element.124), channel_id=1, source_target_pairs={{0,4},{4,0},{8,12},{12,8},{16,20},{20,16},{24,28},{28,24},{1,5},{5... | collective-permute-start | bytes 786440 | tf_op jit(solution)/shard_map/ppermute | solution.py:59
  209.8 47.4 %collective-permute-start.46 = (bf16[512,1024]{1,0:T(8,128)(2,1)}, bf16[512,1024]{1,0:T(8,128)(2,1)}, u32[]{:S(2)}, u32[]{:S(2)}) collective-permute-start(bf16[512,1024]{1,0:T(8,128)(2,1)} %get-tuple-element.129), channel_id=1, source_target_pairs={{0,8},{4,12},{8,0},{12,4},{16,24},{20,28},{24,16},{28,20},{1,9},{5... | collective-permute-start | bytes 3145736 | tf_op jit(solution)/shard_map/ppermute | solution.py:59
  210.2 55.3 %collective-permute-start.52 = (bf16[512,1024]{1,0:T(8,128)(2,1)}, bf16[512,1024]{1,0:T(8,128)(2,1)}, u32[]{:S(2)}, u32[]{:S(2)}) collective-permute-start(bf16[512,1024]{1,0:T(8,128)(2,1)} %get-tuple-element.133), channel_id=1, source_target_pairs={{0,16},{4,20},{8,24},{12,28},{16,0},{20,4},{24,8},{28,12},{1,17},{... | collective-permute-start | bytes 3145736 | tf_op jit(solution)/shard_map/ppermute | solution.py:59
  216.0 31.0 %collective-permute-start.45 = (bf16[256,1024]{1,0:T(8,128)(2,1)}, bf16[256,1024]{1,0:T(8,128)(2,1)}, u32[]{:S(2)}, u32[]{:S(2)}) collective-permute-start(bf16[256,1024]{1,0:T(8,128)(2,1)} %get-tuple-element.125.branch_own), channel_id=1, source_target_pairs={{0,4},{4,0},{8,12},{12,8},{16,20},{20,16},{24,28},{28,24},{1,5},{5... | collective-permute-start | bytes 1572872 | tf_op jit(solution)/shard_map/ppermute | solution.py:59
  245.1 30.2 %collective-permute-start.36 = (bf16[512,768]{1,0:T(8,128)(2,1)}, bf16[512,768]{1,0:T(8,128)(2,1)S(1)}, u32[]{:S(2)}, u32[]{:S(2)}) collective-permute-start(bf16[512,768]{1,0:T(8,128)(2,1)} %get-tuple-element.116), channel_id=1, source_target_pairs={{0,4},{4,0},{8,12},{12,8},{16,20},{20,16},{24,28},{28,24},{1,5},{5... | collective-permute-start | bytes 2359304 | tf_op jit(solution)/shard_map/ppermute | solution.py:59
  245.5 27.4 %collective-permute-start.30 = (bf16[256,1024]{1,0:T(8,128)(2,1)}, bf16[256,1024]{1,0:T(8,128)(2,1)S(1)}, u32[]{:S(2)}, u32[]{:S(2)}) collective-permute-start(bf16[256,1024]{1,0:T(8,128)(2,1)} %copy-done.39), channel_id=1, source_target_pairs={{0,1},{1,2},{2,3},{4,5},{5,6},{6,7},{8,9},{9,10},{10,11},{12,13},{... | collective-permute-start | bytes 1572872 | tf_op jit(solution)/shard_map/ppermute | solution.py:137
  247.0 27.9 %collective-permute-start.33 = (bf16[256,1024]{1,0:T(8,128)(2,1)}, bf16[256,1024]{1,0:T(8,128)(2,1)S(1)}, u32[]{:S(2)}, u32[]{:S(2)}) collective-permute-start(bf16[256,1024]{1,0:T(8,128)(2,1)} %copy-done.33), channel_id=1, source_target_pairs={{1,0},{2,1},{3,2},{5,4},{6,5},{7,6},{9,8},{10,9},{11,10},{13,12},{... | collective-permute-start | bytes 1572872 | tf_op jit(solution)/shard_map/ppermute | solution.py:137
  272.9 49.4 %collective-permute-start.47 = (bf16[640,1024]{1,0:T(8,128)(2,1)S(1)}, bf16[640,1024]{1,0:T(8,128)(2,1)S(1)}, u32[]{:S(2)}, u32[]{:S(2)}) collective-permute-start(bf16[640,1024]{1,0:T(8,128)(2,1)S(1)} %get-tuple-element.130), channel_id=1, source_target_pairs={{0,8},{4,12},{8,0},{12,4},{16,24},{20,28},{24,16},{28,20},{1,9},{5... | collective-permute-start | bytes 3932168 | tf_op jit(solution)/shard_map/ppermute | solution.py:59
  274.9 49.3 %collective-permute-start.53 = (bf16[640,1024]{1,0:T(8,128)(2,1)S(1)}, bf16[640,1024]{1,0:T(8,128)(2,1)S(1)}, u32[]{:S(2)}, u32[]{:S(2)}) collective-permute-start(bf16[640,1024]{1,0:T(8,128)(2,1)S(1)} %get-tuple-element.134), channel_id=1, source_target_pairs={{0,16},{4,20},{8,24},{12,28},{16,0},{20,4},{24,8},{28,12},{1,17},{... | collective-permute-start | bytes 3932168 | tf_op jit(solution)/shard_map/ppermute | solution.py:59
  275.3 49.8 %collective-permute-start.34 = (bf16[256,1024]{1,0:T(8,128)(2,1)S(1)}, bf16[256,1024]{1,0:T(8,128)(2,1)S(1)}, u32[]{:S(2)}, u32[]{:S(2)}) collective-permute-start(bf16[256,1024]{1,0:T(8,128)(2,1)S(1)} %get-tuple-element.157), channel_id=1, source_target_pairs={{1,0},{2,1},{3,2},{5,4},{6,5},{7,6},{9,8},{10,9},{11,10},{13,12},{... | collective-permute-start | bytes 1572872 | tf_op jit(solution)/shard_map/ppermute | solution.py:137
  284.3 45.9 %collective-permute-start.31 = (bf16[256,1024]{1,0:T(8,128)(2,1)S(1)}, bf16[256,1024]{1,0:T(8,128)(2,1)S(1)}, u32[]{:S(2)}, u32[]{:S(2)}) collective-permute-start(bf16[256,1024]{1,0:T(8,128)(2,1)S(1)} %get-tuple-element.158), channel_id=1, source_target_pairs={{0,1},{1,2},{2,3},{4,5},{5,6},{6,7},{8,9},{9,10},{10,11},{12,13},{... | collective-permute-start | bytes 1572872 | tf_op jit(solution)/shard_map/ppermute | solution.py:137
  286.3 27.5 %collective-permute-start.39 = (bf16[128,768]{1,0:T(8,128)(2,1)S(1)}, bf16[128,768]{1,0:T(8,128)(2,1)S(1)}, u32[]{:S(2)}, u32[]{:S(2)}) collective-permute-start(bf16[128,768]{1,0:T(8,128)(2,1)S(1)} %get-tuple-element.120), channel_id=1, source_target_pairs={{0,16},{4,20},{8,24},{12,28},{16,0},{20,4},{24,8},{28,12},{1,17},{... | collective-permute-start | bytes 589832 | tf_op jit(solution)/shard_map/ppermute | solution.py:59
  324.2 23.5 %collective-permute-start.48 = (bf16[320,1024]{1,0:T(8,128)(2,1)S(1)}, bf16[320,1024]{1,0:T(8,128)(2,1)S(1)}, u32[]{:S(2)}, u32[]{:S(2)}) collective-permute-start(bf16[320,1024]{1,0:T(8,128)(2,1)S(1)} %add_convert_fusion.1), channel_id=1, source_target_pairs={{0,16},{4,20},{8,24},{12,28},{16,0},{20,4},{24,8},{28,12},{1,17},{... | collective-permute-start | bytes 1966088 | tf_op jit(solution)/shard_map/ppermute | solution.py:59
  354.6 31.6 %collective-permute-start.56 = (bf16[320,1024]{1,0:T(8,128)(2,1)S(1)}, bf16[320,1024]{1,0:T(8,128)(2,1)S(1)}, u32[]{:S(2)}, u32[]{:S(2)}) collective-permute-start(bf16[320,1024]{1,0:T(8,128)(2,1)S(1)} %fusion.2), channel_id=1, source_target_pairs={{0,1},{3,2},{4,5},{7,6},{8,9},{11,10},{12,13},{15,14},{16,17},{19,... | collective-permute-start | bytes 1966088 | tf_op jit(solution)/shard_map/ppermute | solution.py:832
  357.5 39.6 %collective-permute-start.50 = (bf16[320,1024]{1,0:T(8,128)(2,1)S(1)}, bf16[320,1024]{1,0:T(8,128)(2,1)S(1)}, u32[]{:S(2)}, u32[]{:S(2)}) collective-permute-start(bf16[320,1024]{1,0:T(8,128)(2,1)S(1)} %fusion.3), channel_id=1, source_target_pairs={{0,1},{3,2},{4,5},{7,6},{8,9},{11,10},{12,13},{15,14},{16,17},{19,... | collective-permute-start | bytes 1966088 | tf_op jit(solution)/shard_map/ppermute | solution.py:832
  360.8 37.2 %collective-permute-start.62 = (bf16[256,1024]{1,0:T(8,128)(2,1)S(1)}, bf16[256,1024]{1,0:T(8,128)(2,1)S(1)}, u32[]{:S(2)}, u32[]{:S(2)}) collective-permute-start(bf16[256,1024]{1,0:T(8,128)(2,1)S(1)} %fusion.4), channel_id=1, source_target_pairs={{1,2},{2,1},{5,6},{6,5},{9,10},{10,9},{13,14},{14,13},{17,18},{18,... | collective-permute-start | bytes 1572872 | tf_op jit(solution)/shard_map/ppermute | solution.py:834
  361.7 37.9 %collective-permute-start.66 = (bf16[256,1024]{1,0:T(8,128)(2,1)S(1)}, bf16[256,1024]{1,0:T(8,128)(2,1)S(1)}, u32[]{:S(2)}, u32[]{:S(2)}) collective-permute-start(bf16[256,1024]{1,0:T(8,128)(2,1)S(1)} %fusion.5), channel_id=1, source_target_pairs={{1,2},{2,1},{5,6},{6,5},{9,10},{10,9},{13,14},{14,13},{17,18},{18,... | collective-permute-start | bytes 1572872 | tf_op jit(solution)/shard_map/ppermute | solution.py:834
  399.9 28.7 %collective-permute-start.67 = (bf16[256,1024]{1,0:T(8,128)(2,1)S(1)}, bf16[256,1024]{1,0:T(8,128)(2,1)S(1)}, u32[]{:S(2)}, u32[]{:S(2)}) collective-permute-start(bf16[256,1024]{1,0:T(8,128)(2,1)S(1)} %fusion.9), channel_id=1, source_target_pairs={{1,0},{2,3},{5,4},{6,7},{9,8},{10,11},{13,12},{14,15},{17,16},{18,... | collective-permute-start | bytes 1572872 | tf_op jit(solution)/shard_map/ppermute | solution.py:836
  401.5 41.1 %collective-permute-start.59 = (bf16[320,1024]{1,0:T(8,128)(2,1)S(1)}, bf16[320,1024]{1,0:T(8,128)(2,1)S(1)}, u32[]{:S(2)}, u32[]{:S(2)}) collective-permute-start(bf16[320,1024]{1,0:T(8,128)(2,1)S(1)} %get-tuple-element.147), channel_id=1, source_target_pairs={{1,0},{2,3},{5,4},{6,7},{9,8},{10,11},{13,12},{14,15},{17,16},{18,... | collective-permute-start | bytes 1966088 | tf_op jit(solution)/shard_map/ppermute | solution.py:836
  403.2 48.5 %collective-permute-start.58 = (bf16[320,1024]{1,0:T(8,128)(2,1)S(1)}, bf16[320,1024]{1,0:T(8,128)(2,1)S(1)}, u32[]{:S(2)}, u32[]{:S(2)}) collective-permute-start(bf16[320,1024]{1,0:T(8,128)(2,1)S(1)} %get-tuple-element.149), channel_id=1, source_target_pairs={{1,0},{2,3},{5,4},{6,7},{9,8},{10,11},{13,12},{14,15},{17,16},{18,... | collective-permute-start | bytes 1966088 | tf_op jit(solution)/shard_map/ppermute | solution.py:836
  (122 other events, 1203.7 us)
